TPU v7x, 256 devices: a whole 4x4x8 slice. The times are simulated.
256 devices in a mesh: dp: 8 (over y, x_lo), ctx: 16 (over z, x_hi), tp: 2 (over core).
Axes of the slice: x: 4 (x_hi: 2, x_lo: 2; x = x_hi * 2 + x_lo), y: 4, z: 8, core: 2. Of those that a mesh axis runs over, the one named last changes fastest.
Arguments:
- layer_input: bfloat16 [8, 2048, 8192], P('dp', 'ctx'), may hold values from -6 to 6
- queries: bfloat16 [8, 2048, 4096], P('dp', 'ctx', 'tp'), may hold values from -8 to 8
- keys_values: bfloat16 [2, 8, 2048, 512], P(None, 'dp', 'ctx', 'tp'), may hold values from -8 to 8
- grad_attended: bfloat16 [8, 2048, 4096], P('dp', 'ctx', 'tp'), may hold values from -6 to 6
- grad_layer: bfloat16 [8, 2048, 8192], P('dp', 'ctx'), may hold values from -6 to 6
- block_docs: int32 [8, 16], P('dp'), may hold values from 0 to 3, never falling along the last dimension, each value on 1 to 10 neighbouring positions
- wide_candidates: bfloat16 [2, 8, 4096, 256], P(None, 'dp'), may hold values from -3600 to 3600
- narrow_candidates: bfloat16 [2, 8, 512, 256], P(None, 'dp'), may hold values from -3600 to 3600
- proj_owner: int32 [4], replicated, may hold values from 0 to 7
Outputs:
- attended: bfloat16 [8, 2048, 4096], P('dp', 'ctx', 'tp')
- grad_queries: bfloat16 [8, 2048, 4096], P('dp', 'ctx', 'tp')
- grad_keys_values: bfloat16 [2, 8, 2048, 512], P(None, 'dp', 'ctx', 'tp')
- projected_grads: float32 [8192, 4, 256], P(('dp', 'ctx'), None, 'tp')
Inputs may be any that keep to these rules, and one draw needn't show every extreme that they name: `block_docs`: along each replica's 16 blocks the ids never fall; each document covers 1 to 10 blocks, and one covers exactly 10. `proj_owner`: entries are for the query, key, value and output projections in that order.
All inputs are finite; a program needn't handle non-finite values.
Results may differ from a plain program's by a relative error of at most 0.027.
Values may be sent and summed in bfloat16 or wider, within the bound.
A program may use at most 128 MiB of HBM per device.

v0:
```python
import math

import jax
import jax.numpy as jnp
from jax import lax
from jax.sharding import PartitionSpec as P

HEAD_SIZE = 128
MASK_BLOCK = 128


def from_root(value, axis, source):
    kept = jnp.where(lax.axis_index(axis) == source, value, 0).astype(value.dtype)
    return lax.psum(kept, axis)


def passed_along(block, axis, distance):
    devices = range(lax.axis_size(axis))
    route = [((i - distance) % len(devices), i) for i in devices]
    return lax.ppermute(block, axis, route)


def visible(query_pos, query_doc, key_pos, key_doc):
    return (key_pos[None, :] <= query_pos[:, None]) & (key_doc[None, :] == query_doc[:, None])


def normalize(chosen):
    wide = chosen.astype(jnp.float32)
    return (wide / jnp.sqrt(jnp.sum(wide * wide, axis=0) + 1e-06)).astype(jnp.bfloat16)


def outer_terms(inputs, upstream, shares):
    triple = jnp.einsum("tc,tmr->cmr", inputs, shares[:, :3], preferred_element_type=jnp.float32)
    single = jnp.einsum("tc,tr->cr", upstream, shares[:, 3], preferred_element_type=jnp.float32)
    return jnp.concatenate([triple, single[:, None]], axis=1)


def on_device(
    layer_input,
    queries,
    keys_values,
    grad_attended,
    grad_layer,
    block_docs,
    wide_candidates,
    narrow_candidates,
    proj_owner,
):
    tok_rows = queries.shape[1]
    query_width = queries.shape[2]
    kv_width = keys_values.shape[3]
    groups = kv_width // HEAD_SIZE
    per_group = query_width // HEAD_SIZE // groups
    loop_size = lax.axis_size("ctx")
    replica_count = lax.axis_size("dp")
    loop_index = lax.axis_index("ctx")
    pair_index = lax.axis_index("tp")
    inv_root = 1.0 / math.sqrt(HEAD_SIZE)
    total_rows = tok_rows * loop_size
    offsets = jnp.arange(tok_rows, dtype=jnp.int32)
    token_docs = jnp.repeat(block_docs[0], MASK_BLOCK)
    query_pos = loop_index * tok_rows + offsets
    query_doc = lax.dynamic_slice_in_dim(token_docs, loop_index * tok_rows, tok_rows)
    query_head_rows = queries[0].reshape(tok_rows, groups, per_group, HEAD_SIZE)
    head_gradient = grad_attended[0].reshape(tok_rows, groups, per_group, HEAD_SIZE)

    def choose_basis(candidate, which):
        return normalize(from_root(candidate, "dp", proj_owner[which]))

    basis_query = choose_basis(wide_candidates[0, 0], 0)
    basis_key = choose_basis(narrow_candidates[0, 0], 1)
    basis_value = choose_basis(narrow_candidates[1, 0], 2)
    basis_output = choose_basis(wide_candidates[1, 0], 3)
    kv_piece = lax.all_gather(keys_values, "ctx", axis=2, tiled=True)
    row_max = jnp.full((groups, per_group, tok_rows), -jnp.inf, jnp.float32)
    row_sum = jnp.zeros((groups, per_group, tok_rows), jnp.float32)
    weighted = jnp.zeros((tok_rows, groups, per_group, HEAD_SIZE), jnp.float32)
    key_count = kv_piece.shape[2]
    key_pos = jnp.arange(key_count, dtype=jnp.int32)
    key_doc = token_docs
    visible_mask = visible(query_pos, query_doc, key_pos, key_doc)
    forward_kv_whole = kv_piece[:, 0]
    tile_state = (row_max, row_sum, weighted)
    forward_row_max, forward_row_sum, forward_weighted = tile_state
    key_head_rows = kv_piece[0, 0].reshape(key_count, groups, HEAD_SIZE)
    value_head_rows = kv_piece[1, 0].reshape(key_count, groups, HEAD_SIZE)
    scores = (
        jnp.einsum(
            "hinz,uiz->inhu", query_head_rows, key_head_rows, preferred_element_type=jnp.float32
        )
        * inv_root
    )
    scores = jnp.where(visible_mask[None, None], scores, -jnp.inf)
    new_max = jnp.max(scores, axis=-1)
    safe_max = jnp.where(jnp.isfinite(new_max), new_max, 0.0)
    weights = jnp.exp(scores - safe_max[..., None])
    factor = jnp.exp(forward_row_max - safe_max)
    forward_row_sum = forward_row_sum * factor + jnp.sum(weights, axis=-1)
    blended = jnp.einsum(
        "fxbu,ufh->bfxh",
        weights.astype(jnp.bfloat16),
        value_head_rows,
        preferred_element_type=jnp.float32,
    )
    forward_weighted = forward_weighted * jnp.transpose(factor, (2, 0, 1))[..., None] + blended
    tile_state = (new_max, forward_row_sum, forward_weighted)
    row_max, row_sum, weighted, kv_whole = tile_state + (forward_kv_whole,)
    attended_heads = (weighted / jnp.transpose(row_sum, (2, 0, 1))[..., None]).astype(jnp.bfloat16)
    log_total = row_max + jnp.log(row_sum)
    row_delta = jnp.transpose(
        jnp.sum(head_gradient.astype(jnp.float32) * attended_heads.astype(jnp.float32), axis=-1),
        (1, 2, 0),
    )

    def backward_block(source, query_grads, kv_grads):
        leading_row = source * tok_rows
        kv_block = lax.dynamic_slice_in_dim(kv_whole, leading_row, tok_rows, 1)
        key_pos = leading_row + offsets
        key_doc = lax.dynamic_slice_in_dim(token_docs, leading_row, tok_rows)
        visible_mask = visible(query_pos, query_doc, key_pos, key_doc)
        backward_query_grads = query_grads
        backward_kv_grads = kv_grads
        key_head_rows = kv_block[0].reshape(tok_rows, groups, HEAD_SIZE)
        value_head_rows = kv_block[1].reshape(tok_rows, groups, HEAD_SIZE)
        scores = (
            jnp.einsum(
                "hinz,uiz->inhu", query_head_rows, key_head_rows, preferred_element_type=jnp.float32
            )
            * inv_root
        )
        scores = jnp.where(visible_mask[None, None], scores, -jnp.inf)
        probs = jnp.exp(scores - log_total[..., None])
        grad_probs = jnp.einsum(
            "hinz,uiz->inhu", head_gradient, value_head_rows, preferred_element_type=jnp.float32
        )
        score_gradient = (probs * (grad_probs - row_delta[..., None])).astype(jnp.bfloat16)
        backward_query_grads = (
            backward_query_grads
            + jnp.einsum(
                "fxbu,ufh->bfxh", score_gradient, key_head_rows, preferred_element_type=jnp.float32
            )
            * inv_root
        )
        key_grads = (
            jnp.einsum(
                "wpcx,cwpu->xwu",
                score_gradient,
                query_head_rows,
                preferred_element_type=jnp.float32,
            )
            * inv_root
        )
        value_grads = jnp.einsum(
            "wpcx,cwpu->xwu",
            probs.astype(jnp.bfloat16),
            head_gradient,
            preferred_element_type=jnp.float32,
        )
        backward_kv_grads = backward_kv_grads + jnp.stack(
            [key_grads.reshape(tok_rows, kv_width), value_grads.reshape(tok_rows, kv_width)], axis=0
        )
        return (backward_query_grads, backward_kv_grads)

    query_start = jnp.zeros((tok_rows, groups, per_group, HEAD_SIZE), jnp.float32)

    def pass_grads(step_index, tile_state):
        query_grads, kv_grads = tile_state
        source = (loop_index - step_index) % loop_size
        query_grads, kv_grads = backward_block(source, query_grads, kv_grads)
        kv_grads = passed_along(kv_grads.astype(jnp.bfloat16), "ctx", 1).astype(kv_grads.dtype)
        return (query_grads, kv_grads)

    query_grads, kv_grads = lax.fori_loop(
        0, loop_size, pass_grads, (query_start, jnp.zeros((2, tok_rows, kv_width), jnp.float32))
    )
    attended_flat = attended_heads.reshape(tok_rows, query_width)
    query_flat = query_grads.astype(jnp.bfloat16).reshape(tok_rows, query_width)
    kv_low = kv_grads.astype(jnp.bfloat16)
    local_query = lax.dynamic_slice_in_dim(basis_query, pair_index * query_width, query_width, 0)
    local_key = lax.dynamic_slice_in_dim(basis_key, pair_index * kv_width, kv_width, 0)
    local_value = lax.dynamic_slice_in_dim(basis_value, pair_index * kv_width, kv_width, 0)
    local_output = lax.dynamic_slice_in_dim(basis_output, pair_index * query_width, query_width, 0)
    moments = jnp.stack(
        [
            jnp.dot(query_flat, local_query, preferred_element_type=jnp.float32),
            jnp.dot(kv_low[0], local_key, preferred_element_type=jnp.float32),
            jnp.dot(kv_low[1], local_value, preferred_element_type=jnp.float32),
            jnp.dot(attended_flat, local_output, preferred_element_type=jnp.float32),
        ],
        axis=1,
    )
    shares = lax.psum_scatter(moments.astype(jnp.bfloat16), "tp", scatter_dimension=2, tiled=True)
    grad_factor = 1.0 / math.sqrt(replica_count * total_rows)
    inputs = layer_input[0]
    upstream = grad_layer[0]
    slab_width = inputs.shape[1] // (replica_count * loop_size)
    input_parts = inputs.reshape(tok_rows, replica_count, loop_size, slab_width)
    upstream_parts = upstream.reshape(tok_rows, replica_count, loop_size, slab_width)
    input_mine, upstream_mine = (
        lax.all_to_all(input_parts, "ctx", split_axis=2, concat_axis=0, tiled=True),
        lax.all_to_all(upstream_parts, "ctx", split_axis=2, concat_axis=0, tiled=True),
    )
    input_flat = input_mine.reshape(total_rows, replica_count * slab_width)
    upstream_flat = upstream_mine.reshape(total_rows, replica_count * slab_width)
    all_shares = lax.all_gather(shares, "ctx", axis=0, tiled=True)
    summed = lax.psum_scatter(
        outer_terms(input_flat, upstream_flat, all_shares).astype(jnp.bfloat16),
        "dp",
        scatter_dimension=0,
        tiled=True,
    ).astype(jnp.float32)
    projected_grads = summed * grad_factor
    return (attended_flat[None], query_flat[None], kv_low[:, None], projected_grads)


def solution(mesh):
    return jax.shard_map(
        on_device,
        mesh=mesh,
        in_specs=(
            P("dp", "ctx", None),
            P("dp", "ctx", "tp"),
            P(None, "dp", "ctx", "tp"),
            P("dp", "ctx", "tp"),
            P("dp", "ctx", None),
            P("dp", None),
            P(None, "dp", None, None),
            P(None, "dp", None, None),
            P(),
        ),
        out_specs=(
            P("dp", "ctx", "tp"),
            P("dp", "ctx", "tp"),
            P(None, "dp", "ctx", "tp"),
            P(("dp", "ctx"), None, "tp"),
        ),
        check_vma=False,
    )
```

profile of v0, /device:TPU:6, one launch (start us, length us, event | category | flops | bytes accessed | tf_op | source)
XLA Modules:
  0.0 569.7 jit_solution(9222526607325829353)
XLA Ops:
  14.6 11.6 %all-to-all-start = ((bf16[128,8,16,64]{0,3,1,2:T(8,128)(2,1)}), bf16[128,8,16,64]{0,3,1,2:T(8,128)(2,1)}, u32[]{:S(2)}, u32[]{:S(2)}) async-start(bf16[128,8,16,64]{0,3,1,2:T(8,128)(2,1)} %copy.71), calls=%async_computation | async-start | bytes 4194304 | tf_op jit(solution)/shard_map/all_to_all | solution.py:200
  36.7 93.0 %all-gather.3.cloned.1.call-done = bf16[2,1,2048,256]{2,3,1,0:T(8,128)(2,1)} async-done(((bf16[2,1,128,256]{2,3,1,0:T(8,128)(2,1)}), bf16[2,1,2048,256]{2,3,1,0:T(8,128)(2,1)}) %all-gather.3.cloned.1.call-update) | async-done | bytes 2097168 | tf_op jit(solution)/shard_map/all_gather | solution.py:74
  131.5 7.4 %fusion.19 = (f32[2,8,128]{2,1,0:T(8,128)S(1)}, f32[2,2048,128,8]{2,1,3,0:T(8,128)}) fusion(pred[128,2048]{0,1:T(8,128)(4,1)S(1)} %fusion.47, bf16[2048,2,128,1]{0,2,3,1:T(8,128)(2,1)S(1)} %bitcast.227, bf16[128,2,8,128]{0,3,2,1:T(8,128)(2,1)S(1)} %bitcast.215), kind=kOutput, calls=%fused_computation.29 | convolution fusion | flops 1086322688 | bytes 18620416 | tf_op jit(solution)/shard_map/hinz,uiz->inhu/dot_general | solution.py:88
  138.9 9.2 %fusion.17 = f32[2,8,128]{2,1,0:T(8,128)S(1)} fusion(f32[2,2048,128,8]{2,1,3,0:T(8,128)} %get-tuple-element.417, f32[2,8,128]{2,1,0:T(8,128)S(1)} %is-finite_select_fusion, pred[128,2048]{0,1:T(8,128)(4,1)S(1)} %fusion.47), kind=kLoop, calls=%fused_computation.27 | loop fusion | flops 16775168 | bytes 17055744 | tf_op jit(solution)/shard_map/reduce_sum | solution.py:98
  148.1 8.2 %multiply_reduce_fusion.2 = (f32[128,2,8]{0,2,1:T(8,128)S(1)}, bf16[128,2,8,128]{0,3,2,1:T(8,128)(2,1)S(1)}) fusion(bf16[128,2,8,128]{0,3,2,1:T(8,128)(2,1)S(1)} %bitcast.217, f32[128,2,8]{0,2,1:T(8,128)S(1)} %get-tuple-element.411, bf16[2048,2,128,1]{0,2,3,1:T(8,128)(2,1)S(1)} %bitcast.234, f32[2,2048,128,8]{2,1,3,0:T(8,128)} %get-tuple-element.417, ...), kind=kOutput, calls=%fused_computation.57 | convolution fusion | flops 1092352000 | bytes 19169280 | tf_op jit(solution)/shard_map/fxbu,ufh->bfxh/dot_general | solution.py:99
  156.3 184.7 %while.18 = (s32[]{:T(128)}, f32[128,2,8,128]{0,3,2,1:T(8,128)S(1)}, f32[2,128,256]{1,2,0:T(8,128)S(1)}, s32[]{:T(128)}, bf16[2,2048,256]{1,2,0:T(8,128)(2,1)}, ...) while((s32[]{:T(128)}, ...), condition=%wide.region_4.5_spmd.clone, body=%wide.region_3.4_spmd.clone.sunk | while | flops 338575616 | bytes 11260327 | solution.py:173
  162.8 5.6 collective-permute-done
  192.9 8.6 %collective-permute-done = bf16[2,128,256]{1,2,0:T(8,128)(2,1)S(1)} collective-permute-done((bf16[2,128,256]{1,2,0:T(8,128)(2,1)S(1)}, bf16[2,128,256]{1,2,0:T(8,128)(2,1)S(1)}, u32[]{:S(2)}, u32[]{:S(2)}) %collective-permute-start) | collective-permute-done | bytes 131104 | tf_op jit(solution)/shard_map/while/body/eval_jaxpr/ppermute | solution.py:20
  204.6 9.5 %collective-permute-done = bf16[2,128,256]{1,2,0:T(8,128)(2,1)S(1)} collective-permute-done((bf16[2,128,256]{1,2,0:T(8,128)(2,1)S(1)}, bf16[2,128,256]{1,2,0:T(8,128)(2,1)S(1)}, u32[]{:S(2)}, u32[]{:S(2)}) %collective-permute-start) | collective-permute-done | bytes 131104 | tf_op jit(solution)/shard_map/while/body/eval_jaxpr/ppermute | solution.py:20
  217.3 9.9 %collective-permute-done = bf16[2,128,256]{1,2,0:T(8,128)(2,1)S(1)} collective-permute-done((bf16[2,128,256]{1,2,0:T(8,128)(2,1)S(1)}, bf16[2,128,256]{1,2,0:T(8,128)(2,1)S(1)}, u32[]{:S(2)}, u32[]{:S(2)}) %collective-permute-start) | collective-permute-done | bytes 131104 | tf_op jit(solution)/shard_map/while/body/eval_jaxpr/ppermute | solution.py:20
  230.3 10.1 %collective-permute-done = bf16[2,128,256]{1,2,0:T(8,128)(2,1)S(1)} collective-permute-done((bf16[2,128,256]{1,2,0:T(8,128)(2,1)S(1)}, bf16[2,128,256]{1,2,0:T(8,128)(2,1)S(1)}, u32[]{:S(2)}, u32[]{:S(2)}) %collective-permute-start) | collective-permute-done | bytes 131104 | tf_op jit(solution)/shard_map/while/body/eval_jaxpr/ppermute | solution.py:20
  243.5 9.8 %collective-permute-done = bf16[2,128,256]{1,2,0:T(8,128)(2,1)S(1)} collective-permute-done((bf16[2,128,256]{1,2,0:T(8,128)(2,1)S(1)}, bf16[2,128,256]{1,2,0:T(8,128)(2,1)S(1)}, u32[]{:S(2)}, u32[]{:S(2)}) %collective-permute-start) | collective-permute-done | bytes 131104 | tf_op jit(solution)/shard_map/while/body/eval_jaxpr/ppermute | solution.py:20
  256.4 9.5 %collective-permute-done = bf16[2,128,256]{1,2,0:T(8,128)(2,1)S(1)} collective-permute-done((bf16[2,128,256]{1,2,0:T(8,128)(2,1)S(1)}, bf16[2,128,256]{1,2,0:T(8,128)(2,1)S(1)}, u32[]{:S(2)}, u32[]{:S(2)}) %collective-permute-start) | collective-permute-done | bytes 131104 | tf_op jit(solution)/shard_map/while/body/eval_jaxpr/ppermute | solution.py:20
  269.0 9.2 %collective-permute-done = bf16[2,128,256]{1,2,0:T(8,128)(2,1)S(1)} collective-permute-done((bf16[2,128,256]{1,2,0:T(8,128)(2,1)S(1)}, bf16[2,128,256]{1,2,0:T(8,128)(2,1)S(1)}, u32[]{:S(2)}, u32[]{:S(2)}) %collective-permute-start) | collective-permute-done | bytes 131104 | tf_op jit(solution)/shard_map/while/body/eval_jaxpr/ppermute | solution.py:20
  281.3 8.9 %collective-permute-done = bf16[2,128,256]{1,2,0:T(8,128)(2,1)S(1)} collective-permute-done((bf16[2,128,256]{1,2,0:T(8,128)(2,1)S(1)}, bf16[2,128,256]{1,2,0:T(8,128)(2,1)S(1)}, u32[]{:S(2)}, u32[]{:S(2)}) %collective-permute-start) | collective-permute-done | bytes 131104 | tf_op jit(solution)/shard_map/while/body/eval_jaxpr/ppermute | solution.py:20
  293.4 8.8 %collective-permute-done = bf16[2,128,256]{1,2,0:T(8,128)(2,1)S(1)} collective-permute-done((bf16[2,128,256]{1,2,0:T(8,128)(2,1)S(1)}, bf16[2,128,256]{1,2,0:T(8,128)(2,1)S(1)}, u32[]{:S(2)}, u32[]{:S(2)}) %collective-permute-start) | collective-permute-done | bytes 131104 | tf_op jit(solution)/shard_map/while/body/eval_jaxpr/ppermute | solution.py:20
  305.2 6.0 %collective-permute-done = bf16[2,128,256]{1,2,0:T(8,128)(2,1)S(1)} collective-permute-done((bf16[2,128,256]{1,2,0:T(8,128)(2,1)S(1)}, bf16[2,128,256]{1,2,0:T(8,128)(2,1)S(1)}, u32[]{:S(2)}, u32[]{:S(2)}) %collective-permute-start) | collective-permute-done | bytes 131104 | tf_op jit(solution)/shard_map/while/body/eval_jaxpr/ppermute | solution.py:20
  315.2 5.1 collective-permute-done
  335.3 5.7 collective-permute-done
  353.2 10.1 %reduce-scatter.4.cloned.1.call-done = bf16[128,512]{1,0:T(8,128)(2,1)} async-done(((bf16[256,512]{1,0:T(8,128)(2,1)}), bf16[128,512]{1,0:T(8,128)(2,1)}) %reduce-scatter.4.cloned.1.call-update) | async-done | bytes 131088
  364.3 10.0 %all-to-all-start.1 = ((bf16[128,8,16,64]{0,3,1,2:T(8,128)(2,1)}), bf16[128,8,16,64]{0,3,1,2:T(8,128)(2,1)S(1)}, u32[]{:S(2)}, u32[]{:S(2)}) async-start(bf16[128,8,16,64]{0,3,1,2:T(8,128)(2,1)} %copy.75), calls=%async_computation.1 | async-start | bytes 4194304 | tf_op jit(solution)/shard_map/all_to_all | solution.py:201
  383.6 42.7 %all-to-all-done.1 = bf16[128,8,16,64]{0,3,1,2:T(8,128)(2,1)S(1)} async-done(((bf16[128,8,16,64]{0,3,1,2:T(8,128)(2,1)}), bf16[128,8,16,64]{0,3,1,2:T(8,128)(2,1)S(1)}, u32[]{:S(2)}, u32[]{:S(2)}) %all-to-all-start.1) | async-done | bytes 2097184 | tf_op jit(solution)/shard_map/all_to_all | solution.py:201
  429.0 48.9 %all-gather.5.cloned.1.call-done = bf16[2048,4,128]{0,2,1:T(8,128)(2,1)} async-done(((bf16[128,4,128]{0,2,1:T(8,128)(2,1)}), bf16[2048,4,128]{0,2,1:T(8,128)(2,1)}) %all-gather.5.cloned.1.call-update) | async-done | bytes 2097168 | tf_op jit(solution)/shard_map/all_gather | solution.py:205
  487.4 73.6 %all-reduce.5.cloned.1.call-done = bf16[512,4,128]{2,1,0:T(4,128)(2,1)} async-done(((bf16[512,4,128]{2,1,0:T(4,128)(2,1)}), bf16[512,4,128]{2,1,0:T(4,128)(2,1)}) %all-reduce.5.cloned.1.call-update) | async-done | bytes 524304
  (285 shorter events, 127.5 us)
Async XLA Ops:
  8.0 121.8 %all-gather.3.cloned.1.call-start = ((), (), s32[]{:S(2)}) async-start(), calls=%async_computation.3 | async-start | bytes 2228224 | tf_op jit(solution)/shard_map/all_gather | solution.py:74
  14.6 349.7 %all-to-all-start = ((bf16[128,8,16,64]{0,3,1,2:T(8,128)(2,1)}), bf16[128,8,16,64]{0,3,1,2:T(8,128)(2,1)}, u32[]{:S(2)}, u32[]{:S(2)}) async-start(bf16[128,8,16,64]{0,3,1,2:T(8,128)(2,1)} %copy.71), calls=%async_computation | async-start | bytes 4194304 | tf_op jit(solution)/shard_map/all_to_all | solution.py:200
  26.1 315.1 %all-reduce.7.cloned.1.call-start = ((), (), s32[]{:S(2)}) async-start(), calls=%async_computation.7 | async-start | bytes 9437184 | tf_op jit(solution)/shard_map/psum | solution.py:14
  34.7 328.6 %reduce-scatter.4.cloned.1.call-start = ((), (), s32[]{:S(2)}) async-start(), calls=%async_computation.5 | async-start | bytes 393216
  158.8 9.5 %collective-permute-start = (bf16[2,128,256]{1,2,0:T(8,128)(2,1)S(1)}, bf16[2,128,256]{1,2,0:T(8,128)(2,1)S(1)}, u32[]{:S(2)}, u32[]{:S(2)}) collective-permute-start(bf16[2,128,256]{1,2,0:T(8,128)(2,1)S(1)} %fusion.112), channel_id=1, source_target_pairs={{30,0},{0,2},{2,4},{4,6},{6,8},{8,10},{10,12},{12,14},{14,16},{16,... | collective-permute-start | bytes 393224 | tf_op jit(solution)/shard_map/while/body/eval_jaxpr/ppermute | solution.py:20
  171.0 6.5 %collective-permute-start = (bf16[2,128,256]{1,2,0:T(8,128)(2,1)S(1)}, bf16[2,128,256]{1,2,0:T(8,128)(2,1)S(1)}, u32[]{:S(2)}, u32[]{:S(2)}) collective-permute-start(bf16[2,128,256]{1,2,0:T(8,128)(2,1)S(1)} %fusion.112), channel_id=1, source_target_pairs={{30,0},{0,2},{2,4},{4,6},{6,8},{8,10},{10,12},{12,14},{14,16},{16,... | collective-permute-start | bytes 393224 | tf_op jit(solution)/shard_map/while/body/eval_jaxpr/ppermute | solution.py:20
  180.1 7.0 %collective-permute-start = (bf16[2,128,256]{1,2,0:T(8,128)(2,1)S(1)}, bf16[2,128,256]{1,2,0:T(8,128)(2,1)S(1)}, u32[]{:S(2)}, u32[]{:S(2)}) collective-permute-start(bf16[2,128,256]{1,2,0:T(8,128)(2,1)S(1)} %fusion.112), channel_id=1, source_target_pairs={{30,0},{0,2},{2,4},{4,6},{6,8},{8,10},{10,12},{12,14},{14,16},{16,... | collective-permute-start | bytes 393224 | tf_op jit(solution)/shard_map/while/body/eval_jaxpr/ppermute | solution.py:20
  189.7 11.9 %collective-permute-start = (bf16[2,128,256]{1,2,0:T(8,128)(2,1)S(1)}, bf16[2,128,256]{1,2,0:T(8,128)(2,1)S(1)}, u32[]{:S(2)}, u32[]{:S(2)}) collective-permute-start(bf16[2,128,256]{1,2,0:T(8,128)(2,1)S(1)} %fusion.112), channel_id=1, source_target_pairs={{30,0},{0,2},{2,4},{4,6},{6,8},{8,10},{10,12},{12,14},{14,16},{16,... | collective-permute-start | bytes 393224 | tf_op jit(solution)/shard_map/while/body/eval_jaxpr/ppermute | solution.py:20
  204.1 10.1 %collective-permute-start = (bf16[2,128,256]{1,2,0:T(8,128)(2,1)S(1)}, bf16[2,128,256]{1,2,0:T(8,128)(2,1)S(1)}, u32[]{:S(2)}, u32[]{:S(2)}) collective-permute-start(bf16[2,128,256]{1,2,0:T(8,128)(2,1)S(1)} %fusion.112), channel_id=1, source_target_pairs={{30,0},{0,2},{2,4},{4,6},{6,8},{8,10},{10,12},{12,14},{14,16},{16,... | collective-permute-start | bytes 393224 | tf_op jit(solution)/shard_map/while/body/eval_jaxpr/ppermute | solution.py:20
  216.7 10.5 %collective-permute-start = (bf16[2,128,256]{1,2,0:T(8,128)(2,1)S(1)}, bf16[2,128,256]{1,2,0:T(8,128)(2,1)S(1)}, u32[]{:S(2)}, u32[]{:S(2)}) collective-permute-start(bf16[2,128,256]{1,2,0:T(8,128)(2,1)S(1)} %fusion.112), channel_id=1, source_target_pairs={{30,0},{0,2},{2,4},{4,6},{6,8},{8,10},{10,12},{12,14},{14,16},{16,... | collective-permute-start | bytes 393224 | tf_op jit(solution)/shard_map/while/body/eval_jaxpr/ppermute | solution.py:20
  229.8 10.6 %collective-permute-start = (bf16[2,128,256]{1,2,0:T(8,128)(2,1)S(1)}, bf16[2,128,256]{1,2,0:T(8,128)(2,1)S(1)}, u32[]{:S(2)}, u32[]{:S(2)}) collective-permute-start(bf16[2,128,256]{1,2,0:T(8,128)(2,1)S(1)} %fusion.112), channel_id=1, source_target_pairs={{30,0},{0,2},{2,4},{4,6},{6,8},{8,10},{10,12},{12,14},{14,16},{16,... | collective-permute-start | bytes 393224 | tf_op jit(solution)/shard_map/while/body/eval_jaxpr/ppermute | solution.py:20
  242.9 10.3 %collective-permute-start = (bf16[2,128,256]{1,2,0:T(8,128)(2,1)S(1)}, bf16[2,128,256]{1,2,0:T(8,128)(2,1)S(1)}, u32[]{:S(2)}, u32[]{:S(2)}) collective-permute-start(bf16[2,128,256]{1,2,0:T(8,128)(2,1)S(1)} %fusion.112), channel_id=1, source_target_pairs={{30,0},{0,2},{2,4},{4,6},{6,8},{8,10},{10,12},{12,14},{14,16},{16,... | collective-permute-start | bytes 393224 | tf_op jit(solution)/shard_map/while/body/eval_jaxpr/ppermute | solution.py:20
  255.8 10.0 %collective-permute-start = (bf16[2,128,256]{1,2,0:T(8,128)(2,1)S(1)}, bf16[2,128,256]{1,2,0:T(8,128)(2,1)S(1)}, u32[]{:S(2)}, u32[]{:S(2)}) collective-permute-start(bf16[2,128,256]{1,2,0:T(8,128)(2,1)S(1)} %fusion.112), channel_id=1, source_target_pairs={{30,0},{0,2},{2,4},{4,6},{6,8},{8,10},{10,12},{12,14},{14,16},{16,... | collective-permute-start | bytes 393224 | tf_op jit(solution)/shard_map/while/body/eval_jaxpr/ppermute | solution.py:20
  268.4 9.8 %collective-permute-start = (bf16[2,128,256]{1,2,0:T(8,128)(2,1)S(1)}, bf16[2,128,256]{1,2,0:T(8,128)(2,1)S(1)}, u32[]{:S(2)}, u32[]{:S(2)}) collective-permute-start(bf16[2,128,256]{1,2,0:T(8,128)(2,1)S(1)} %fusion.112), channel_id=1, source_target_pairs={{30,0},{0,2},{2,4},{4,6},{6,8},{8,10},{10,12},{12,14},{14,16},{16,... | collective-permute-start | bytes 393224 | tf_op jit(solution)/shard_map/while/body/eval_jaxpr/ppermute | solution.py:20
  280.8 9.5 %collective-permute-start = (bf16[2,128,256]{1,2,0:T(8,128)(2,1)S(1)}, bf16[2,128,256]{1,2,0:T(8,128)(2,1)S(1)}, u32[]{:S(2)}, u32[]{:S(2)}) collective-permute-start(bf16[2,128,256]{1,2,0:T(8,128)(2,1)S(1)} %fusion.112), channel_id=1, source_target_pairs={{30,0},{0,2},{2,4},{4,6},{6,8},{8,10},{10,12},{12,14},{14,16},{16,... | collective-permute-start | bytes 393224 | tf_op jit(solution)/shard_map/while/body/eval_jaxpr/ppermute | solution.py:20
  292.8 9.3 %collective-permute-start = (bf16[2,128,256]{1,2,0:T(8,128)(2,1)S(1)}, bf16[2,128,256]{1,2,0:T(8,128)(2,1)S(1)}, u32[]{:S(2)}, u32[]{:S(2)}) collective-permute-start(bf16[2,128,256]{1,2,0:T(8,128)(2,1)S(1)} %fusion.112), channel_id=1, source_target_pairs={{30,0},{0,2},{2,4},{4,6},{6,8},{8,10},{10,12},{12,14},{14,16},{16,... | collective-permute-start | bytes 393224 | tf_op jit(solution)/shard_map/while/body/eval_jaxpr/ppermute | solution.py:20
  304.7 6.5 %collective-permute-start = (bf16[2,128,256]{1,2,0:T(8,128)(2,1)S(1)}, bf16[2,128,256]{1,2,0:T(8,128)(2,1)S(1)}, u32[]{:S(2)}, u32[]{:S(2)}) collective-permute-start(bf16[2,128,256]{1,2,0:T(8,128)(2,1)S(1)} %fusion.112), channel_id=1, source_target_pairs={{30,0},{0,2},{2,4},{4,6},{6,8},{8,10},{10,12},{12,14},{14,16},{16,... | collective-permute-start | bytes 393224 | tf_op jit(solution)/shard_map/while/body/eval_jaxpr/ppermute | solution.py:20
  313.8 6.5 %collective-permute-start = (bf16[2,128,256]{1,2,0:T(8,128)(2,1)S(1)}, bf16[2,128,256]{1,2,0:T(8,128)(2,1)S(1)}, u32[]{:S(2)}, u32[]{:S(2)}) collective-permute-start(bf16[2,128,256]{1,2,0:T(8,128)(2,1)S(1)} %fusion.112), channel_id=1, source_target_pairs={{30,0},{0,2},{2,4},{4,6},{6,8},{8,10},{10,12},{12,14},{14,16},{16,... | collective-permute-start | bytes 393224 | tf_op jit(solution)/shard_map/while/body/eval_jaxpr/ppermute | solution.py:20
  322.9 6.8 %collective-permute-start = (bf16[2,128,256]{1,2,0:T(8,128)(2,1)S(1)}, bf16[2,128,256]{1,2,0:T(8,128)(2,1)S(1)}, u32[]{:S(2)}, u32[]{:S(2)}) collective-permute-start(bf16[2,128,256]{1,2,0:T(8,128)(2,1)S(1)} %fusion.112), channel_id=1, source_target_pairs={{30,0},{0,2},{2,4},{4,6},{6,8},{8,10},{10,12},{12,14},{14,16},{16,... | collective-permute-start | bytes 393224 | tf_op jit(solution)/shard_map/while/body/eval_jaxpr/ppermute | solution.py:20
  332.3 8.7 %collective-permute-start = (bf16[2,128,256]{1,2,0:T(8,128)(2,1)S(1)}, bf16[2,128,256]{1,2,0:T(8,128)(2,1)S(1)}, u32[]{:S(2)}, u32[]{:S(2)}) collective-permute-start(bf16[2,128,256]{1,2,0:T(8,128)(2,1)S(1)} %fusion.112), channel_id=1, source_target_pairs={{30,0},{0,2},{2,4},{4,6},{6,8},{8,10},{10,12},{12,14},{14,16},{16,... | collective-permute-start | bytes 393224 | tf_op jit(solution)/shard_map/while/body/eval_jaxpr/ppermute | solution.py:20
  364.3 62.0 %all-to-all-start.1 = ((bf16[128,8,16,64]{0,3,1,2:T(8,128)(2,1)}), bf16[128,8,16,64]{0,3,1,2:T(8,128)(2,1)S(1)}, u32[]{:S(2)}, u32[]{:S(2)}) async-start(bf16[128,8,16,64]{0,3,1,2:T(8,128)(2,1)} %copy.75), calls=%async_computation.1 | async-start | bytes 4194304 | tf_op jit(solution)/shard_map/all_to_all | solution.py:201
  374.3 103.6 %all-gather.5.cloned.1.call-start = ((), (), s32[]{:S(2)}) async-start(), calls=%async_computation.4 | async-start | bytes 2228224 | tf_op jit(solution)/shard_map/all_gather | solution.py:205
  375.1 186.0 %all-reduce.5.cloned.1.call-start = ((), (), s32[]{:S(2)}) async-start(), calls=%async_computation.6 | async-start | bytes 1048576
  482.9 79.6 %copy-start.1 = (s32[1,16]{1,0:T(1,128)S(1)}, s32[1,16]{1,0:T(1,128)}, u32[]{:S(2)}) copy-start(s32[1,16]{1,0:T(1,128)} %param.16) | copy-start | bytes 196
  (12 other events, 120.2 us)
Sparse Core Ops, SparseCore 0:
  11.9 117.8 all-gather.2
  348.3 14.9 reduce-scatter.3
  378.5 99.4 all-gather.4
Sparse Core Ops, SparseCore 1:
  34.8 273.8 all-reduce.6
  484.2 76.8 all-reduce.4
where the time goes:
time: 573 us; the launch traced here: 570 us
  waiting for transfers between devices  389 us (68%)
  matrix products  49.9 us (9%)
  local copies, waits for them, and re-layouts  49.6 us (9%)
  starting transfers between devices  38.1 us (7%)
  other arithmetic  22.8 us (4%)
  between operations  18.8 us (3%)
    ppermute x16, waiting for transfers between devices, passed_along(): return lax.ppermute(block, axis, route)  120 us
    all_gather x1, waiting for transfers between devices, on_device(): kv_piece = lax.all_gather(keys_values, 'ctx', axis=2, tiled=True)  93 us
    unnamed x7, waiting for transfers between devices  83.8 us
    all_gather x1, waiting for transfers between devices, on_device(): all_shares = lax.all_gather(shares, 'ctx', axis=0, tiled=True)  48.9 us
    all_to_all x1, waiting for transfers between devices, on_device(): lax.all_to_all(upstream_parts, 'ctx', split_axis=2, concat_axis=0, tiled=...  42.7 us
    ppermute x16, starting transfers between devices, passed_along(): return lax.ppermute(block, axis, route)  16.3 us
    unnamed x36, local copies, waits for them, and re-layouts  14.5 us
    slice x16, local copies, waits for them, and re-layouts, backward_block(): value_head_rows = kv_block[1].reshape(tok_rows, groups, HEAD_SIZE)  14.1 us
  transfers between devices with their start and end apart: 23, of which 21 were waited for; matrix products, arithmetic and copies ran while one was open for 19% of the time, Pallas kernels for 0%

commit v1 on v0

v1 whole, which is shorter than its diff:
```python
import math

import jax
import jax.numpy as jnp
from jax import lax
from jax.experimental import pallas as pl
from jax.experimental.pallas import tpu as pltpu
from jax.sharding import PartitionSpec as P

HEAD = 128
BLOCK = 128
LONGEST = 10
NEG = -1e30
MESH = pl.DeviceIdType.MESH
BF16 = jnp.bfloat16
F32 = jnp.float32
INV_ROOT = 1.0 / math.sqrt(HEAD)

NX = 2
NY = 4
NZ = 8
PLANE = NX * NX * NY


def dot(a, b, dims=((1,), (0,))):
    return lax.dot_general(a, b, (dims, ((), ())), preferred_element_type=F32)


def kernel(
    x_ref, q_ref, kv_ref, do_ref, gl_ref, docs_ref, wide_ref, narrow_ref, owner_ref,
    att_out, gq_out, gkv_out, proj_out,
    qf, dof, qs, dos, qt, dot_, kvg, w, mx, den, delta, ot, dqt, attf, gqf,
    dsend, dacc, xrecv, tin, ext, kvo,
    bxw, bxn, byw, byn, basw, basn, xr, xt, pm, sx, rx, mm, rs, rr, ssq, rssq,
    load_sem, out_sem,
    kv_recv, kv_send_z, kv_send_x, kv_send_9,
    x_send, x_recv, t_send, t_recv, ext_send, ext_recv,
    bx_send, bx_recv, by_send, by_recv, ring_send, ring_recv,
    a_send, a_recv, sib_send, sib_recv, m_send, m_recv, r_send, r_recv,
):
    d = lax.axis_index("dp")
    c = lax.axis_index("ctx")
    t = lax.axis_index("tp")
    y, xl = lax.div(d, NX), lax.rem(d, NX)
    z, xh = lax.div(c, NX), lax.rem(c, NX)
    plane = d * NX + xh
    partner = (d, c + 1 - 2 * xh, t)
    above = (d, c + NX, t)
    below = (d, c - NX, t)
    sibling = (d, c, 1 - t)

    def local(src, dst, sem):
        return pltpu.make_async_copy(src, dst, sem)

    def remote(src, dst, send, recv, device):
        return pltpu.make_async_remote_copy(
            src_ref=src, dst_ref=dst, send_sem=send, recv_sem=recv,
            device_id=device, device_id_type=MESH,
        )

    def arrived(dst, recv):
        remote(dst, dst, recv, recv, sibling).wait_recv()

    def left(src, send):
        remote(src, src, send, send, sibling).wait_send()

    def loop(low, high, body):
        def step(i, carry):
            body(i)
            return carry
        lax.fori_loop(low, high, step, 0)

    q_load = local(q_ref.at[0], qf, load_sem.at[0])
    do_load = local(do_ref.at[0], dof, load_sem.at[1])
    kv_load = local(kv_ref.at[:, 0], kvg.at[0], load_sem.at[2])
    wide_mine = wide_ref.at[:, 0, pl.ds(pl.multiple_of(t * 2048 + z * 256, 256), 256), :]
    narrow_mine = narrow_ref.at[:, 0, pl.ds(pl.multiple_of(t * 256 + z * 32, 32), 32), :]
    w_load = local(wide_mine, bxw.at[xl], load_sem.at[3])
    n_load = local(narrow_mine, bxn.at[xl], load_sem.at[4])
    kv_load.start()
    q_load.start()
    do_load.start()
    w_load.start()
    n_load.start()

    barrier = pltpu.get_barrier_semaphore()

    def greet(device):
        pl.semaphore_signal(barrier, inc=1, device_id=device, device_id_type=MESH)

    def plane_device(k):
        other = lax.rem(plane + k, PLANE)
        return other, (lax.div(other, NX), z * NX + lax.rem(other, NX), t)

    loop(1, PLANE, lambda k: greet(plane_device(k)[1]))

    def greet_column(k):
        zz = lax.rem(z + k, NZ)
        greet((d, zz * NX, t))
        greet((d, zz * NX + 1, t))

    loop(1, NZ, greet_column)
    greet(sibling)
    pl.semaphore_wait(barrier, (PLANE - 1) + 2 * (NZ - 1) + 1)

    def forward_kv(s):
        slot = 2 * s

        @pl.when((s <= 3) & (z <= NZ - 2))
        def _():
            remote(kvg.at[slot], kvg.at[slot + 2], kv_send_z.at[s], kv_recv.at[slot + 2], above).start()

        @pl.when(xh == 0)
        def _():
            remote(kvg.at[slot], kvg.at[slot + 1], kv_send_x.at[s], kv_recv.at[slot + 1], partner).start()

        @pl.when((xh == 1) & (s >= 1))
        def _():
            remote(kvg.at[slot], kvg.at[slot - 1], kv_send_x.at[s], kv_recv.at[slot - 1], partner).start()

        @pl.when((xh == 1) & (s == 4) & (z <= NZ - 2))
        def _():
            remote(kvg.at[8], kvg.at[9], kv_send_9.at[0], kv_recv.at[9], (d, c + 1, t)).start()

    kv_load.wait()
    forward_kv(0)

    across = (d + 1 - 2 * xl, c, t)
    bx_copies = (
        remote(wide_mine, bxw.at[xl], bx_send.at[0], bx_recv.at[0], across),
        remote(narrow_mine, bxn.at[xl], bx_send.at[1], bx_recv.at[1], across),
    )
    for copy in bx_copies:
        copy.start()

    q_load.wait()
    do_load.wait()

    def split_heads(h):
        g, i = lax.div(h, 8), lax.rem(h, 8)
        columns = pl.ds(pl.multiple_of(h * HEAD, HEAD), HEAD)
        rows = pl.ds(pl.multiple_of(i * HEAD, HEAD), HEAD)
        tile = qf[:, columns]
        qs[g, rows, :] = tile
        qt[g, :, rows] = tile.T
        tile = dof[:, columns]
        dos[g, rows, :] = tile
        dot_[g, :, rows] = tile.T

    loop(0, 16, split_heads)

    def score(j, diagonal=False):
        if not diagonal:
            same = docs_ref[0, c] == docs_ref[0, c - j]
            bias = jnp.where(same, 0.0, NEG).astype(F32)
        for g in range(2):
            key = kvg[j, 0, :, g * HEAD:(g + 1) * HEAD]
            s = dot(key, qt[g]) * INV_ROOT
            if diagonal:
                rows = lax.broadcasted_iota(jnp.int32, s.shape, 0)
                lanes = lax.broadcasted_iota(jnp.int32, s.shape, 1) & (BLOCK - 1)
                s = jnp.where(rows <= lanes, s, NEG)
                mx[g] = jnp.max(s, axis=0, keepdims=True)
            else:
                s = s + bias
                mx[g] = jnp.maximum(mx[g], jnp.max(s, axis=0, keepdims=True))
            w[j, g] = s

    score(0, True)

    def forward_step(s):
        @pl.when(z >= s)
        def _():
            arrived(kvg.at[2 * s], kv_recv.at[2 * s])
            forward_kv(s)
            score(2 * s)

        @pl.when(z + xh >= s)
        def _():
            arrived(kvg.at[2 * s - 1], kv_recv.at[2 * s - 1])
            score(2 * s - 1)

    loop(1, 3, forward_step)

    for copy in bx_copies:
        copy.wait_recv()
    w_load.wait()
    n_load.wait()
    owners = [owner_ref[m] for m in range(4)]
    for m, n in ((0, 0), (1, 3)):
        byw[y, m] = bxw[lax.rem(owners[n], NX), m]
    for m, n in ((0, 1), (1, 2)):
        byn[y, m] = bxn[lax.rem(owners[n], NX), m]

    def y_copies(k):
        device = (lax.rem(y + k, NY) * NX + xl, c, t)
        return (
            remote(byw.at[y], byw.at[y], by_send.at[k, 0], by_recv.at[y, 0], device),
            remote(byn.at[y], byn.at[y], by_send.at[k, 1], by_recv.at[y, 1], device),
        )

    for k in range(1, NY):
        for copy in y_copies(k):
            copy.start()

    loop(3, 5, forward_step)

    @pl.when(z + xh >= 5)
    def _():
        arrived(kvg.at[9], kv_recv.at[9])
        score(9)

    def a_copy(source, k):
        other, device = plane_device(k)
        columns = pl.ds(pl.multiple_of(other * 512, 512), 512)
        return remote(source.at[0, :, columns], xr.at[t, plane], a_send.at[k], a_recv.at[plane], device)

    mine = pl.ds(pl.multiple_of(plane * 512, 512), 512)

    @pl.when(t == 0)
    def _():
        loop(1, PLANE, lambda k: a_copy(x_ref, k).start())
        local(x_ref.at[0, :, mine], xr.at[0, plane], load_sem.at[5]).start()

    @pl.when(t == 1)
    def _():
        loop(1, PLANE, lambda k: a_copy(gl_ref, k).start())
        local(gl_ref.at[0, :, mine], xr.at[1, plane], load_sem.at[5]).start()

    def y_arrived(k):
        yy = lax.rem(y + k, NY)
        arrived(byw.at[yy], by_recv.at[yy, 0])
        arrived(byn.at[yy], by_recv.at[yy, 1])

    for k in range(1, NY):
        y_arrived(k)
    for m, n in ((0, 0), (1, 3)):
        basw[m, pl.ds(pl.multiple_of(z * 256, 256), 256), :] = byw[lax.div(owners[n], NX), m]
    for m, n in ((0, 1), (1, 2)):
        basn[m, pl.ds(pl.multiple_of(z * 32, 32), 32), :] = byn[lax.div(owners[n], NX), m]

    z_up = (d, lax.rem(z + 1, NZ) * NX + xh, t)
    z_down = (d, lax.rem(z + NZ - 1, NZ) * NX + xh, t)

    def eighth(p):
        p = lax.rem(p + 2 * NZ, NZ)
        return (
            basw.at[:, pl.ds(pl.multiple_of(p * 256, 256), 256), :],
            basn.at[:, pl.ds(pl.multiple_of(p * 32, 32), 32), :],
        )

    def ring_copies(k):
        copies = []
        for way, device, p in ((0, z_up, z - k), (1, z_down, z + k)):
            if way == 1 and k == 3:
                continue
            for n, ref in enumerate(eighth(p)):
                copies.append(remote(ref, ref, ring_send.at[way, k, n], ring_recv.at[way, k, n], device))
        return copies

    def ring_arrived(k):
        for way, p in ((0, z - 1 - k), (1, z + 1 + k)):
            if way == 1 and k == 3:
                continue
            for n, ref in enumerate(eighth(p)):
                arrived(ref, ring_recv.at[way, k, n])

    def ring_step(k):
        if k >= 1:
            ring_arrived(k - 1)
        if k <= 3:
            for copy in ring_copies(k):
                copy.start()

    ring_step(0)

    den[...] = jnp.zeros_like(den)
    ot[...] = jnp.zeros_like(ot)
    dqt[...] = jnp.zeros_like(dqt)

    def weigh(j):
        for g in range(2):
            value = kvg[j, 1, :, g * HEAD:(g + 1) * HEAD]
            p = jnp.exp(w[j, g] - mx[g])
            w[j, g] = p
            den[g] += jnp.sum(p, axis=0, keepdims=True)
            ot[g] += dot(value, p.astype(BF16), ((0,), (0,)))

    loop(0, jnp.minimum(c, LONGEST - 1) + 1, weigh)
    for g in range(2):
        den[g] = 1.0 / den[g]

    def finish_heads(h):
        g, i = lax.div(h, 8), lax.rem(h, 8)
        columns = pl.ds(pl.multiple_of(h * HEAD, HEAD), HEAD)
        rows = pl.ds(pl.multiple_of(i * HEAD, HEAD), HEAD)
        low = (ot[g, :, rows] * den[g, :, rows]).astype(BF16).astype(F32)
        delta[g, :, rows] = jnp.sum(low * dot_[g, :, rows].astype(F32), axis=0, keepdims=True)
        attf[:, columns] = low.T.astype(BF16)

    loop(0, 16, finish_heads)
    att_store = local(attf, att_out.at[0], out_sem.at[0])
    att_store.start()
    ring_step(1)

    def backward(j, store):
        for g in range(2):
            columns = slice(g * HEAD, (g + 1) * HEAD)
            key = kvg[j, 0, :, columns]
            value = kvg[j, 1, :, columns]
            p = w[j, g] * den[g]
            ds = (p * (dot(value, dot_[g]) - delta[g])).astype(BF16)
            dqt[g] += dot(key, ds, ((0,), (0,)))
            store(0, columns, dot(ds, qs[g]) * INV_ROOT)
            store(1, columns, dot(p.astype(BF16), dos[g]))

    def chain(s):
        @pl.when(z >= s)
        def _():
            @pl.when((xh == 0) | (s >= 1))
            def _():
                arrived(xrecv.at[s], x_recv.at[s])
                dacc[s] += xrecv[s].astype(F32)

            @pl.when((s == 4) & (xh == 1) & (z <= NZ - 2))
            def _():
                arrived(ext, ext_recv.at[0])
                dacc[s] += ext[...].astype(F32)

            @pl.when((s <= 3) & (z <= NZ - 2))
            def _():
                arrived(tin.at[s], t_recv.at[s])
                dacc[s] += tin[s].astype(F32)

            @pl.when(s >= 1)
            def _():
                dsend[2 * s] = dacc[s].astype(BF16)
                remote(dsend.at[2 * s], tin.at[s - 1], t_send.at[s], t_recv.at[s - 1], below).start()

    def backward_step(i):
        s = 4 - i

        @pl.when(z + xh >= s + 1)
        def _():
            def store(which, columns, val):
                dsend[2 * s + 1, which, :, columns] = val.astype(BF16)

            backward(2 * s + 1, store)

            @pl.when(xh == 1)
            def _():
                remote(dsend.at[2 * s + 1], xrecv.at[s], x_send.at[s], x_recv.at[s], partner).start()

            @pl.when((xh == 0) & (s <= 3))
            def _():
                remote(dsend.at[2 * s + 1], xrecv.at[s + 1], x_send.at[s], x_recv.at[s + 1], partner).start()

            @pl.when((xh == 0) & (s == 4))
            def _():
                remote(dsend.at[9], ext, ext_send.at[0], ext_recv.at[0], (d, c - 1, t)).start()

        @pl.when(z >= s)
        def _():
            def store(which, columns, val):
                dacc[s, which, :, columns] = val

            backward(2 * s, store)

        @pl.when(i >= 1)
        def _():
            chain(s + 1)

    loop(0, 2, backward_step)
    ring_step(2)
    loop(2, 4, backward_step)
    ring_step(3)
    loop(4, 5, backward_step)

    def finish_grads(h):
        g, i = lax.div(h, 8), lax.rem(h, 8)
        columns = pl.ds(pl.multiple_of(h * HEAD, HEAD), HEAD)
        rows = pl.ds(pl.multiple_of(i * HEAD, HEAD), HEAD)
        gqf[:, columns] = (dqt[g, :, rows] * INV_ROOT).T.astype(BF16)

    loop(0, 16, finish_grads)
    gq_store = local(gqf, gq_out.at[0], out_sem.at[1])
    gq_store.start()

    local(xr.at[t, plane], xr.at[t, plane], load_sem.at[5]).wait()

    def a_arrived(k):
        other = lax.rem(plane + k, PLANE)
        arrived(xr.at[t, other], a_recv.at[other])

    loop(1, PLANE, a_arrived)
    hand_over = remote(xr.at[t], xr.at[t], sib_send.at[0], sib_recv.at[0], sibling)
    hand_over.start()
    ring_step(4)

    low_half = pl.ds(pl.multiple_of(t * 128, 128), 128)
    high_half = pl.ds(pl.multiple_of((1 - t) * 128, 128), 128)

    def give(part, pairs):
        for n, (rows, basis) in enumerate(pairs):
            pm[part, n] = dot(rows, basis)
            sx[part, n] = pm[part, n, :, high_half].astype(BF16)
        copy = remote(sx.at[part], rx.at[part], sib_send.at[1 + part], sib_recv.at[1 + part], sibling)
        copy.start()
        return copy

    def m_copy(part, k):
        ref = mm.at[part, plane]
        return remote(ref, ref, m_send.at[part, k], m_recv.at[part, plane], plane_device(k)[1])

    def spread(part):
        arrived(rx.at[part], sib_recv.at[1 + part])
        for n in range(2):
            share = pm[part, n, :, low_half] + rx[part, n].astype(F32)
            mm[part, plane, :, n * 128:(n + 1) * 128] = share.astype(BF16)
        loop(1, PLANE, lambda k: m_copy(part, k).start())

    give_a = give(0, ((attf[...], basw[1]), (gqf[...], basw[0])))
    for m, (ref, n) in enumerate(((basw, 0), (basn, 0), (basn, 1), (basw, 1))):
        wide = ref[n].astype(F32)
        ssq[m:m + 1, :] = jnp.sum(wide * wide, axis=0, keepdims=True)
    give_s = remote(ssq, rssq, sib_send.at[3], sib_recv.at[3], sibling)
    give_s.start()
    spread(0)

    chain(0)
    kvo[...] = dacc[0].astype(BF16)
    kv_store = local(kvo, gkv_out.at[:, 0], out_sem.at[2])
    kv_store.start()
    give_b = give(1, ((kvo[0], basn[0]), (kvo[1], basn[1])))
    spread(1)

    def turn(a):
        def one(p):
            for n in range(4):
                xt[a, n * 128:(n + 1) * 128, pl.ds(pl.multiple_of(p * 128, 128), 128)] = (
                    xr[a, p, :, n * 128:(n + 1) * 128].T
                )
        loop(0, PLANE, one)

    turn(t)
    arrived(xr.at[1 - t], sib_recv.at[0])
    turn(1 - t)

    def m_arrived(part):
        def one(k):
            other = lax.rem(plane + k, PLANE)
            arrived(mm.at[part, other], m_recv.at[part, other])
        loop(1, PLANE, one)

    def piece_device(k):
        zz = xh * 4 + lax.div(k, 2)
        return zz, lax.rem(k, 2)

    def reduce_out(part):
        def one(k):
            zz, xx = piece_device(k)
            own = (zz == z) & (xx == xh)

            @pl.when(own)
            def _():
                rr[part, z] = rs[part, k]

            @pl.when(jnp.logical_not(own))
            def _():
                remote(
                    rs.at[part, k], rr.at[part, z], r_send.at[part, k], r_recv.at[part, z],
                    (d, zz * NX + xx, t),
                ).start()

        loop(0, 8, one)

    def outer(part):
        m_arrived(part)

        def one(n):
            rows = pl.ds(pl.multiple_of(n * 128, 128), 128)
            if part == 0:
                out = dot(xt[1, rows, :], mm[0, :, :, 0:128].reshape(PLANE * 128, 128))
                gq = dot(xt[0, rows, :], mm[0, :, :, 128:256].reshape(PLANE * 128, 128))
                val = jnp.concatenate([out, gq], axis=1)
            else:
                val = dot(xt[0, rows, :], mm[1].reshape(PLANE * 128, 256))
            rs[part, pl.ds(2 * n, 2)] = val.astype(BF16).reshape(2, 64, 256)

        loop(0, 4, one)
        reduce_out(part)

    outer(0)
    outer(1)

    source = lax.div(z, 4)

    def r_arrived(part):
        def one(zz):
            @pl.when(jnp.logical_not((source == xh) & (zz == z)))
            def _():
                arrived(rr.at[part, zz], r_recv.at[part, zz])
        loop(0, NZ, one)

    arrived(rssq, sib_recv.at[3])
    rssq[...] = lax.rsqrt(ssq[...] + rssq[...] + 1e-06) * (1.0 / 128.0)
    for part, places in ((0, (3, 0)), (1, (1, 2))):
        r_arrived(part)
        total = jnp.sum(rr[part].astype(F32), axis=0)
        for n, m in enumerate(places):
            proj_out[:, m, :] = total[:, n * 128:(n + 1) * 128] * rssq[m:m + 1, low_half]

    att_store.wait()
    gq_store.wait()
    kv_store.wait()

    def kv_left(s):
        @pl.when((z >= s) & (s <= 3) & (z <= NZ - 2))
        def _():
            left(kvg.at[0], kv_send_z.at[s])

        @pl.when((z >= s) & ((xh == 0) | (s >= 1)))
        def _():
            left(kvg.at[0], kv_send_x.at[s])

        @pl.when((z >= s) & (s >= 1))
        def _():
            left(dsend.at[0], t_send.at[s])

        @pl.when((z + xh >= s + 1) & ((xh == 1) | (s <= 3)))
        def _():
            left(dsend.at[0], x_send.at[s])

    loop(0, 5, kv_left)

    @pl.when((xh == 1) & (z >= 4) & (z <= NZ - 2))
    def _():
        left(kvg.at[0], kv_send_9.at[0])

    @pl.when((xh == 0) & (z >= 5))
    def _():
        left(dsend.at[0], ext_send.at[0])

    for copy in bx_copies:
        copy.wait_send()
    for k in range(1, NY):
        for copy in y_copies(k):
            copy.wait_send()
    for k in range(4):
        for copy in ring_copies(k):
            copy.wait_send()

    def plane_left(k):
        left(xr.at[0, 0], a_send.at[k])
        left(mm.at[0, 0], m_send.at[0, k])
        left(mm.at[1, 0], m_send.at[1, k])

    loop(1, PLANE, plane_left)
    for copy in (hand_over, give_a, give_b, give_s):
        copy.wait_send()

    def reduce_left(k):
        zz, xx = piece_device(k)

        @pl.when(jnp.logical_not((zz == z) & (xx == xh)))
        def _():
            left(rs.at[0, 0], r_send.at[0, k])
            left(rs.at[1, 0], r_send.at[1, k])

    loop(0, 8, reduce_left)


def on_device(*args):
    dma = pltpu.SemaphoreType.DMA
    vmem = pltpu.VMEM
    scratch = [
        vmem((128, 2048), BF16), vmem((128, 2048), BF16),
        vmem((2, 1024, 128), BF16), vmem((2, 1024, 128), BF16),
        vmem((2, 128, 1024), BF16), vmem((2, 128, 1024), BF16),
        vmem((LONGEST, 2, 128, 256), BF16),
        vmem((LONGEST, 2, 128, 1024), F32),
        vmem((2, 1, 1024), F32), vmem((2, 1, 1024), F32), vmem((2, 1, 1024), F32),
        vmem((2, 128, 1024), F32), vmem((2, 128, 1024), F32),
        vmem((128, 2048), BF16), vmem((128, 2048), BF16),
        vmem((LONGEST, 2, 128, 256), BF16), vmem((5, 2, 128, 256), F32),
        vmem((5, 2, 128, 256), BF16), vmem((4, 2, 128, 256), BF16),
        vmem((2, 128, 256), BF16), vmem((2, 128, 256), BF16),
        vmem((2, 2, 256, 256), BF16), vmem((2, 2, 32, 256), BF16),
        vmem((4, 2, 256, 256), BF16), vmem((4, 2, 32, 256), BF16),
        vmem((2, 2048, 256), BF16), vmem((2, 256, 256), BF16),
        vmem((2, PLANE, 128, 512), BF16), vmem((2, 512, 2048), BF16),
        vmem((2, 2, 128, 256), F32), vmem((2, 2, 128, 128), BF16), vmem((2, 2, 128, 128), BF16),
        vmem((2, PLANE, 128, 256), BF16),
        vmem((2, 8, 64, 256), BF16), vmem((2, 8, 64, 256), BF16),
        vmem((4, 256), F32), vmem((4, 256), F32),
        dma((6,)), dma((3,)),
        dma((10,)), dma((4,)), dma((5,)), dma((1,)),
        dma((5,)), dma((5,)), dma((5,)), dma((4,)), dma((1,)), dma((1,)),
        dma((2,)), dma((2,)), dma((4, 2)), dma((4, 2)), dma((2, 4, 2)), dma((2, 4, 2)),
        dma((PLANE,)), dma((PLANE,)), dma((4,)), dma((4,)),
        dma((2, PLANE)), dma((2, PLANE)), dma((2, 8)), dma((2, 8)),
    ]
    hbm = pl.BlockSpec(memory_space=pl.ANY)
    smem = pl.BlockSpec(memory_space=pltpu.SMEM)
    return pl.pallas_call(
        kernel,
        out_shape=(
            jax.ShapeDtypeStruct((1, 128, 2048), BF16),
            jax.ShapeDtypeStruct((1, 128, 2048), BF16),
            jax.ShapeDtypeStruct((2, 1, 128, 256), BF16),
            jax.ShapeDtypeStruct((64, 4, 128), F32),
        ),
        in_specs=[hbm] * 5 + [smem] + [hbm] * 2 + [smem],
        out_specs=(hbm, hbm, hbm, pl.BlockSpec(memory_space=pltpu.VMEM)),
        scratch_shapes=scratch,
        compiler_params=pltpu.CompilerParams(
            collective_id=0, has_side_effects=True, vmem_limit_bytes=60 * 1024 * 1024
        ),
        cost_estimate=pl.CostEstimate(flops=7_000_000_000, bytes_accessed=12_000_000, transcendentals=3_000_000),
    )(*args)


def solution(mesh):
    return jax.shard_map(
        on_device,
        mesh=mesh,
        in_specs=(
            P("dp", "ctx", None),
            P("dp", "ctx", "tp"),
            P(None, "dp", "ctx", "tp"),
            P("dp", "ctx", "tp"),
            P("dp", "ctx", None),
            P("dp", None),
            P(None, "dp", None, None),
            P(None, "dp", None, None),
            P(),
        ),
        out_specs=(
            P("dp", "ctx", "tp"),
            P("dp", "ctx", "tp"),
            P(None, "dp", "ctx", "tp"),
            P(("dp", "ctx"), None, "tp"),
        ),
        check_vma=False,
    )
```

time: 573 us -> 149 us (0.26)
  waiting for transfers between devices: 389 us -> 0 us
  Pallas kernels: 0 us -> 140 us
  matrix products: 49.9 us -> 0 us
  local copies, waits for them, and re-layouts: 49.6 us -> 5.12 us
  starting transfers between devices: 38.1 us -> 0 us
  other arithmetic: 22.8 us -> 0 us
  between operations: 18.8 us -> 0.66 us
    all_gather x2 -> x0, waiting for transfers between devices: 142 us -> none  [the longest x1 93 us: on_device(): kv_piece = lax.all_gather(keys_values, 'ctx', axis=2, tiled=True)]
    pallas_call x0 -> x1, Pallas kernels: none -> 140 us  [on_device(): pl.pallas_call(kernel, out_shape=(jax.ShapeDtypeStruct((1, 128, 2048), BF...]
    ppermute x16 -> x0, waiting for transfers between devices: 120 us -> none  [passed_along(): return lax.ppermute(block, axis, route)]
    unnamed x7 -> x0, waiting for transfers between devices: 83.8 us -> none
    dot_general x88 -> x0, matrix products: 49.9 us -> none  [the longest x1 8.16 us: on_device(): jnp.einsum('fxbu,ufh->bfxh', weights.astype(jnp.bfloat16), value_head_row...]
    all_to_all x2 -> x0, waiting for transfers between devices: 42.7 us -> none  [the longest x1 42.7 us: on_device(): lax.all_to_all(upstream_parts, 'ctx', split_axis=2, concat_axis=0, tiled=...]
    all_to_all x2 -> x0, starting transfers between devices: 21.6 us -> none  [the longest x1 11.6 us: on_device(): lax.all_to_all(input_parts, 'ctx', split_axis=2, concat_axis=0, tiled=True)]
    slice x18 -> x0, local copies, waits for them, and re-layouts: 16.5 us -> none  [the longest x16 14.1 us: backward_block(): value_head_rows = kv_block[1].reshape(tok_rows, groups, HEAD_SIZE)]
  transfers between devices with their start and end apart: 23 -> 0, of which waited for: 21 -> 0; matrix products, arithmetic and copies ran while one was open for 19% -> 0% of each run, Pallas kernels for 0% -> 0%
where the time goes in v1:
time: 149 us; the launch traced here: 146 us
  Pallas kernels  140 us (94%)
  local copies, waits for them, and re-layouts  5.12 us (3%)
    pallas_call x1, Pallas kernels, on_device(): pl.pallas_call(kernel, out_shape=(jax.ShapeDtypeStruct((1, 128, 2048), BF...  140 us
    unnamed x8, local copies, waits for them, and re-layouts  5.12 us

profile of v1, /device:TPU:6, one launch (start us, length us, event | category | flops | bytes accessed | tf_op | source)
XLA Modules:
  0.0 146.1 jit_solution(13496943853112773903)
XLA Ops:
  0.6 140.3 %shard_map.120 = (bf16[1,128,2048]{2,1,0:T(8,128)(2,1)}, bf16[1,128,2048]{2,1,0:T(8,128)(2,1)}, bf16[2,1,128,256]{3,2,1,0:T(8,128)(2,1)}, f32[64,4,128]{2,1,0:T(4,128)}) custom-call(bf16[1,128,8192]{2,1,0:T(8,128)(2,1)} %x_ref.1, bf16[1,128,2048]{2,1,0:T(8,128)(2,1)} %q_ref.1, bf16[2,1,128,256]{3,2,1,0:T(8,128)(2,1)} %kv_ref.1, ...), custom_call_target="tpu_custom_call" | custom-call | flops 7000000000 | bytes 12000000 | tf_op jit(solution)/shard_map/pallas_call | solution.py:605
  141.0 0.0 copy-start.1
  141.0 0.0 copy-start
  141.0 1.9 %copy.17 = bf16[1,128,2048]{2,1,0:T(8,128)(2,1)} copy(bf16[1,128,2048]{2,1,0:T(8,128)(2,1)} %get-tuple-element.8) | data formatting | bytes 1048576
  142.9 1.9 %copy.18 = bf16[1,128,2048]{2,1,0:T(8,128)(2,1)} copy(bf16[1,128,2048]{2,1,0:T(8,128)(2,1)} %get-tuple-element.9) | data formatting | bytes 1048576
  144.8 0.0 copy-done.1
  144.8 0.7 copy.19
  145.5 0.0 copy-done
  145.5 0.7 copy.20
Async XLA Ops:
  141.0 3.8 %copy-start.1 = (bf16[2,1,128,256]{3,2,1,0:T(8,128)(2,1)S(1)}, bf16[2,1,128,256]{3,2,1,0:T(8,128)(2,1)}, u32[]{:S(2)}) copy-start(bf16[2,1,128,256]{3,2,1,0:T(8,128)(2,1)} %get-tuple-element.10) | copy-start | bytes 393220
  141.0 4.5 %copy-start = (f32[64,4,128]{2,1,0:T(4,128)S(1)}, f32[64,4,128]{2,1,0:T(4,128)}, u32[]{:S(2)}) copy-start(f32[64,4,128]{2,1,0:T(4,128)} %get-tuple-element.11) | copy-start | bytes 393220

commit v2 on v1

v2 whole, which is shorter than its diff:
```python
import math

import jax
import jax.numpy as jnp
from jax import lax
from jax.experimental import pallas as pl
from jax.experimental.pallas import tpu as pltpu
from jax.sharding import PartitionSpec as P

HEAD = 128
BLOCK = 128
LONGEST = 10
NEG = -1e30
MESH = pl.DeviceIdType.MESH
BF16 = jnp.bfloat16
F32 = jnp.float32
INV_ROOT = 1.0 / math.sqrt(HEAD)

NX = 2
NY = 4
NZ = 8
PLANE = NX * NX * NY


def dot(a, b, dims=((1,), (0,))):
    return lax.dot_general(a, b, (dims, ((), ())), preferred_element_type=F32)


def kernel(
    x_ref, q_ref, kv_ref, do_ref, gl_ref, docs_ref, wide_ref, narrow_ref, owner_ref,
    att_out, gq_out, gkv_out, proj_out,
    qf, dof, qs, dos, qt, dot_, kvg, w, mx, den, delta, ot, dqt,
    dsend, dacc, xrecv, tin, ext,
    bx, pk, by, bas, xr, xt, pm, sx, rx, mm, rs, rr, ssq, rssq,
    load_sem,
    kv_recv, kv_send_z, kv_send_x, kv_send_9,
    x_send, x_recv, t_send, t_recv, ext_send, ext_recv,
    bx_send, bx_recv, by_send, by_recv, ring_send, ring_recv, yf_send, yf_recv,
    a_send, a_recv, sib_send, sib_recv, m_send, m_recv, r_send, r_recv,
):
    d = lax.axis_index("dp")
    c = lax.axis_index("ctx")
    t = lax.axis_index("tp")
    y, xl = lax.div(d, NX), lax.rem(d, NX)
    z, xh = lax.div(c, NX), lax.rem(c, NX)
    plane = d * NX + xh
    odd, odd_z = lax.rem(y, 2), lax.rem(z, 2)
    side = xh + odd_z * (1 - 2 * xh)
    partner = (d, c + 1 - 2 * xh, t)
    above = (d, c + NX, t)
    below = (d, c - NX, t)
    sibling = (d, c, 1 - t)

    def local(src, dst, sem):
        return pltpu.make_async_copy(src, dst, sem)

    def remote(src, dst, send, recv, device):
        return pltpu.make_async_remote_copy(
            src_ref=src, dst_ref=dst, send_sem=send, recv_sem=recv,
            device_id=device, device_id_type=MESH,
        )

    def arrived(dst, recv):
        remote(dst, dst, recv, recv, sibling).wait_recv()

    def left(src, send):
        remote(src, src, send, send, sibling).wait_send()

    def loop(low, high, body):
        def step(i, carry):
            body(i)
            return carry
        lax.fori_loop(low, high, step, 0)

    q_load = local(q_ref.at[0], qf, load_sem.at[0])
    do_load = local(do_ref.at[0], dof, load_sem.at[1])
    kv_load = local(kv_ref.at[:, 0], kvg.at[0], load_sem.at[2])

    def mine_of(half):
        return (
            wide_ref.at[half, 0, pl.ds(pl.multiple_of(t * 2048 + z * 256, 256), 256), :],
            narrow_ref.at[half, 0, pl.ds(pl.multiple_of(t * 256 + z * 32, 32), 32), :],
        )

    b_loads = []
    for half in range(2):
        for n, (source, rows) in enumerate(zip(mine_of(half), (pl.ds(0, 256), pl.ds(256, 32)))):
            b_loads.append(local(source, bx.at[half, xl, rows], load_sem.at[3 + 2 * half + n]))
    kv_load.start()
    q_load.start()
    do_load.start()
    for copy in b_loads:
        copy.start()

    barrier = pltpu.get_barrier_semaphore()

    def greet(device):
        pl.semaphore_signal(barrier, inc=1, device_id=device, device_id_type=MESH)

    def plane_device(k):
        other = lax.rem(plane + k, PLANE)
        return other, (lax.div(other, NX), z * NX + lax.rem(other, NX), t)

    loop(1, PLANE, lambda k: greet(plane_device(k)[1]))

    def greet_column(k):
        zz = lax.rem(z + k, NZ)
        greet((d, zz * NX, t))
        greet((d, zz * NX + 1, t))

    loop(1, NZ, greet_column)
    greet(sibling)

    def split_heads(h):
        g, i = lax.div(h, 8), lax.rem(h, 8)
        columns = pl.ds(pl.multiple_of(h * HEAD, HEAD), HEAD)
        rows = pl.ds(pl.multiple_of(i * HEAD, HEAD), HEAD)
        tile = qf[:, columns]
        qs[g, rows, :] = tile
        qt[g, :, rows] = tile.T
        tile = dof[:, columns]
        dos[g, rows, :] = tile
        dot_[g, :, rows] = tile.T

    q_load.wait()
    do_load.wait()
    loop(0, 16, split_heads)
    kv_load.wait()

    def score(j, diagonal=False):
        if not diagonal:
            same = docs_ref[0, c] == docs_ref[0, c - j]
            bias = jnp.where(same, 0.0, NEG).astype(F32)
        for g in range(2):
            key = kvg[j, 0, :, g * HEAD:(g + 1) * HEAD]
            s = dot(key, qt[g]) * INV_ROOT
            if diagonal:
                rows = lax.broadcasted_iota(jnp.int32, s.shape, 0)
                lanes = lax.broadcasted_iota(jnp.int32, s.shape, 1) & (BLOCK - 1)
                s = jnp.where(rows <= lanes, s, NEG)
                mx[g] = jnp.max(s, axis=0, keepdims=True)
            else:
                s = s + bias
                mx[g] = jnp.maximum(mx[g], jnp.max(s, axis=0, keepdims=True))
            w[j, g] = s

    score(0, True)
    pl.semaphore_wait(barrier, (PLANE - 1) + 2 * (NZ - 1) + 1)

    def forward_kv(s, h):
        slot = 2 * s

        def to(dst, send, device):
            remote(kvg.at[slot, h], kvg.at[dst, h], send, kv_recv.at[dst, h], device).start()

        @pl.when((s <= 3) & (z <= NZ - 2))
        def _():
            to(slot + 2, kv_send_z.at[s, h], above)

        @pl.when(xh == 0)
        def _():
            to(slot + 1, kv_send_x.at[s, h], partner)

        @pl.when((xh == 1) & (s >= 1))
        def _():
            to(slot - 1, kv_send_x.at[s, h], partner)

        @pl.when((xh == 1) & (s == 4) & (z <= NZ - 2))
        def _():
            to(9, kv_send_9.at[h], (d, c + 1, t))

    forward_kv(0, 0)
    forward_kv(0, 1)

    x_pair = (d + 1 - 2 * xl, c, t)
    x_other = (d + 1 - 2 * xl, c + 1 - 2 * xh, t)
    owners = [owner_ref[m] for m in range(4)]
    bx_copies = []
    for half, device in enumerate((x_pair, x_other)):
        for n, (source, rows) in enumerate(zip(mine_of(half), (pl.ds(0, 256), pl.ds(256, 32)))):
            bx_copies.append(
                remote(source, bx.at[half, xl, rows], bx_send.at[half, n], bx_recv.at[half, n], device)
            )
    for copy in bx_copies:
        copy.start()

    def columns_of(p):
        p = p + odd_z * (1 - 2 * lax.rem(p, 2))
        return pl.ds(pl.multiple_of(p * 512, 512), 512)

    def send_inputs(steps):
        for core, source in enumerate((x_ref, gl_ref)):
            @pl.when(t == core)
            def _():
                for k in steps:
                    other, device = plane_device(k)
                    remote(
                        source.at[0, :, columns_of(other)], xr.at[core, plane], a_send.at[k], a_recv.at[plane], device
                    ).start()
                if 4 in steps:
                    local(source.at[0, :, columns_of(plane)], xr.at[core, plane], load_sem.at[7]).start()

    send_inputs((4, 8, 12))

    def y_device(k):
        return (lax.rem(y + k, NY) * NX + xl, c, t)

    by_copies = [
        remote(pk.at[odd if k == 2 else 1 - odd], by.at[y], by_send.at[k], by_recv.at[y], y_device(k))
        for k in range(1, NY)
    ]

    def pick_x():
        for copy in b_loads:
            copy.wait()
        for copy in bx_copies:
            copy.wait_recv()
        for half, (wide, narrow) in enumerate(((0, 1), (3, 2))):
            pk[half, 0:256] = bx[half, lax.rem(owners[wide], NX), 0:256]
            pk[half, 256:288] = bx[half, lax.rem(owners[narrow], NX), 256:288]
        for copy in by_copies:
            copy.start()

    def pick_y():
        by[y] = pk[odd]
        for k in range(1, NY):
            yy = lax.rem(y + k, NY)
            arrived(by.at[yy], by_recv.at[yy])
        wide = jnp.where(odd == 0, owners[0], owners[3])
        narrow = jnp.where(odd == 0, owners[1], owners[2])
        bas[odd, z, 0:256] = by[lax.div(wide, NX), 0:256]
        bas[odd, z, 256:288] = by[lax.div(narrow, NX), 256:288]

    z_up = (d, lax.rem(z + 1, NZ) * NX + xh, t)
    z_down = (d, lax.rem(z + NZ - 1, NZ) * NX + xh, t)
    LOW, HIGH = pl.ds(0, 144), pl.ds(144, 144)

    def part_of(p):
        return lax.rem(p + 2 * NZ, NZ)

    def ring_parts(k, ways):
        parts = []
        for way, device, p in ways:
            ref = bas.at[odd, part_of(p)]
            if k == 3:
                ref = ref.at[(LOW, HIGH)[way]]
            parts.append((ref, ring_send.at[way, k], ring_recv.at[way, k], device))
        return parts

    def ring_copies(k):
        parts = ring_parts(k, ((0, z_up, z - k), (1, z_down, z + k)))
        return [remote(ref, ref, send, recv, device) for ref, send, recv, device in parts]

    def y_forward(p):
        p = part_of(p)
        return [
            remote(ref, ref, yf_send.at[n, p], yf_recv.at[n, p], y_device(k))
            for n, (ref, k) in enumerate(((bas.at[odd, p, LOW], 1), (bas.at[odd, p, HIGH], 3)))
        ]

    def ring_step(k):
        if k >= 1:
            for ref, _, recv, _ in ring_parts(k - 1, ((0, z_up, z - k), (1, z_down, z + k))):
                arrived(ref, recv)
        if k <= 3:
            for copy in ring_copies(k):
                copy.start()
        for p in ((z - k, z + k) if 1 <= k <= 3 else (z + k,)):
            for copy in y_forward(p):
                copy.start()

    def odd_slot(j):
        arrived(kvg.at[j, 0], kv_recv.at[j, 0])
        score(j)

    def forward_step(s):
        @pl.when(z >= s)
        def _():
            arrived(kvg.at[2 * s, 0], kv_recv.at[2 * s, 0])
            forward_kv(s, 0)
            score(2 * s)
            arrived(kvg.at[2 * s, 1], kv_recv.at[2 * s, 1])
            forward_kv(s, 1)

        @pl.when((s >= 2) & (z + xh >= s - 1))
        def _():
            odd_slot(2 * s - 3)

        @pl.when(s == 2)
        def _():
            pick_x()

    loop(1, 5, forward_step)
    pick_y()
    ring_step(0)

    def last_slots(s):
        @pl.when(z + xh >= s)
        def _():
            odd_slot(2 * s - 1)

    loop(4, 6, last_slots)

    def odd_values(s):
        @pl.when(z + xh >= s)
        def _():
            arrived(kvg.at[2 * s - 1, 1], kv_recv.at[2 * s - 1, 1])

    loop(1, 6, odd_values)
    ring_step(1)

    send_inputs((1, 2, 3, 5, 6, 7))

    den[...] = jnp.zeros_like(den)
    ot[...] = jnp.zeros_like(ot)
    dqt[...] = jnp.zeros_like(dqt)

    def weigh(j):
        for g in range(2):
            value = kvg[j, 1, :, g * HEAD:(g + 1) * HEAD]
            p = jnp.exp(w[j, g] - mx[g])
            w[j, g] = p
            den[g] += jnp.sum(p, axis=0, keepdims=True)
            ot[g] += dot(value, p.astype(BF16), ((0,), (0,)))

    loop(0, jnp.minimum(c, LONGEST - 1) + 1, weigh)
    for g in range(2):
        den[g] = 1.0 / den[g]

    def finish_heads(h):
        g, i = lax.div(h, 8), lax.rem(h, 8)
        columns = pl.ds(pl.multiple_of(h * HEAD, HEAD), HEAD)
        rows = pl.ds(pl.multiple_of(i * HEAD, HEAD), HEAD)
        low = (ot[g, :, rows] * den[g, :, rows]).astype(BF16)
        wide = low.astype(F32) * dot_[g, :, rows].astype(F32)
        delta[g, :, rows] = jnp.sum(wide, axis=0, keepdims=True)
        att_out[0, :, columns] = low.T

    loop(0, 16, finish_heads)
    ring_step(2)

    def backward(j, store):
        for g in range(2):
            columns = slice(g * HEAD, (g + 1) * HEAD)
            key = kvg[j, 0, :, columns]
            value = kvg[j, 1, :, columns]
            p = w[j, g] * den[g]
            ds = (p * (dot(value, dot_[g]) - delta[g])).astype(BF16)
            dqt[g] += dot(key, ds, ((0,), (0,)))
            store(0, columns, dot(ds, qs[g]) * INV_ROOT)
            store(1, columns, dot(p.astype(BF16), dos[g]))

    def chain(s):
        @pl.when(z >= s)
        def _():
            @pl.when((xh == 0) | (s >= 1))
            def _():
                arrived(xrecv.at[s], x_recv.at[s])
                dacc[s] += xrecv[s].astype(F32)

            @pl.when((s == 4) & (xh == 1) & (z <= NZ - 2))
            def _():
                arrived(ext, ext_recv.at[0])
                dacc[s] += ext[...].astype(F32)

            for h in range(2):
                @pl.when((s <= 3) & (z <= NZ - 2))
                def _():
                    arrived(tin.at[s, h], t_recv.at[s, h])
                    dacc[s, h] += tin[s, h].astype(F32)

                @pl.when(s >= 1)
                def _():
                    dsend[2 * s, h] = dacc[s, h].astype(BF16)
                    remote(
                        dsend.at[2 * s, h], tin.at[s - 1, h], t_send.at[s, h], t_recv.at[s - 1, h], below
                    ).start()

    def backward_step(i):
        s = 4 - i

        @pl.when(z + xh >= s + 1)
        def _():
            def store(which, columns, val):
                dsend[2 * s + 1, which, :, columns] = val.astype(BF16)

            backward(2 * s + 1, store)

            @pl.when(xh == 1)
            def _():
                remote(dsend.at[2 * s + 1], xrecv.at[s], x_send.at[s], x_recv.at[s], partner).start()

            @pl.when((xh == 0) & (s <= 3))
            def _():
                remote(dsend.at[2 * s + 1], xrecv.at[s + 1], x_send.at[s], x_recv.at[s + 1], partner).start()

            @pl.when((xh == 0) & (s == 4))
            def _():
                remote(dsend.at[9], ext, ext_send.at[0], ext_recv.at[0], (d, c - 1, t)).start()

        @pl.when(z >= s)
        def _():
            def store(which, columns, val):
                dacc[s, which, :, columns] = val

            backward(2 * s, store)

        @pl.when(i >= 3)
        def _():
            chain(s + 3)

        @pl.when(i == 1)
        def _():
            ring_step(3)

        @pl.when(i == 3)
        def _():
            ring_step(4)

    loop(0, 5, backward_step)
    chain(2)
    send_inputs((9, 10, 11, 13, 14, 15))

    def finish_grads(h):
        g, i = lax.div(h, 8), lax.rem(h, 8)
        columns = pl.ds(pl.multiple_of(h * HEAD, HEAD), HEAD)
        rows = pl.ds(pl.multiple_of(i * HEAD, HEAD), HEAD)
        gq_out[0, :, columns] = (dqt[g, :, rows] * INV_ROOT).astype(BF16).T

    loop(0, 16, finish_grads)
    chain(1)

    for n in range(2):
        for p in range(NZ):
            arrived(bas.at[1 - odd, p, (LOW, HIGH)[n]], yf_recv.at[n, p])

    low_half = pl.ds(pl.multiple_of(t * 128, 128), 128)
    high_half = pl.ds(pl.multiple_of((1 - t) * 128, 128), 128)

    def give(part, pairs):
        for n, (rows, basis) in enumerate(pairs):
            pm[part, n] = dot(rows, basis)
            sx[part, n] = pm[part, n, :, high_half].astype(BF16)
        copy = remote(sx.at[part], rx.at[part], sib_send.at[1 + part], sib_recv.at[1 + part], sibling)
        copy.start()
        return copy

    quad = xl * NX + xh

    def m_parts(part, n, stage, k):
        if n == stage:
            other = lax.rem(quad + k, 4)
            device = (y * NX + lax.div(other, NX), z * NX + lax.rem(other, NX), t)
            mine, theirs = quad, other
        else:
            other = lax.rem(y + k, NY)
            device = (other * NX + xl, c, t)
            mine, theirs = y, other
        lanes = pl.ds(n * 128, 128)

        def ref(at):
            if stage == 0:
                return mm.at[part, y, at, :, lanes] if n == 0 else mm.at[part, at, quad, :, lanes]
            return mm.at[part, at, :, :, lanes] if n == 0 else mm.at[part, :, at, :, lanes]

        return (
            lambda: remote(
                ref(mine), ref(mine), m_send.at[part, n, stage, k], m_recv.at[part, n, stage, mine], device
            ),
            (ref(theirs), m_recv.at[part, n, stage, theirs]),
        )

    def m_start(part, stage):
        for n in range(2):
            loop(1, 4, lambda k: m_parts(part, n, stage, k)[0]().start())

    def m_arrived(part, stage):
        for n in range(2):
            loop(1, 4, lambda k: arrived(*m_parts(part, n, stage, k)[1]))

    def spread(part):
        arrived(rx.at[part], sib_recv.at[1 + part])
        for n in range(2):
            share = pm[part, n, :, low_half] + rx[part, n].astype(F32)
            mm[part, y, quad, :, n * 128:(n + 1) * 128] = share.astype(BF16)
        m_start(part, 0)

    def wide_basis(half):
        return bas[half, :, 0:256, :].reshape(NZ * 256, 256)

    def narrow_basis(half):
        return bas[half, :, 256:288, :].reshape(NZ * 32, 256)

    give_a = give(0, ((att_out[0], wide_basis(1)), (gq_out[0], wide_basis(0))))
    spread(0)
    chain(0)
    for h in range(2):
        gkv_out[h, 0] = dacc[0, h].astype(BF16)
    give_b = give(1, ((gkv_out[0, 0], narrow_basis(0)), (gkv_out[1, 0], narrow_basis(1))))
    spread(1)
    m_arrived(0, 0)
    m_start(0, 1)
    for m, value in enumerate((wide_basis(0), narrow_basis(0), narrow_basis(1), wide_basis(1))):
        wide = value.astype(F32)
        ssq[m:m + 1, :] = jnp.sum(wide * wide, axis=0, keepdims=True)
    give_s = remote(ssq, rssq, sib_send.at[3], sib_recv.at[3], sibling)
    give_s.start()


    local(xr.at[t, plane], xr.at[t, plane], load_sem.at[7]).wait()

    def a_arrived(k):
        other = lax.rem(plane + k, PLANE)
        arrived(xr.at[t, other], a_recv.at[other])

    loop(1, PLANE, a_arrived)
    hand_over = remote(xr.at[t], xr.at[t], sib_send.at[0], sib_recv.at[0], sibling)
    hand_over.start()

    def turn(a):
        def one(p):
            for n in range(4):
                xt[a, n * 128:(n + 1) * 128, pl.ds(pl.multiple_of(p * 128, 128), 128)] = (
                    xr[a, p, :, n * 128:(n + 1) * 128].T
                )
        loop(0, PLANE, one)

    turn(t)
    m_arrived(1, 0)
    m_start(1, 1)
    arrived(xr.at[1 - t], sib_recv.at[0])
    turn(1 - t)

    def piece_device(k):
        zz = side * 4 + lax.div(k, 2)
        return zz, lax.rem(k, 2)

    def reduce_out(part):
        def one(k):
            zz, xx = piece_device(k)
            own = (zz == z) & (xx == xh)

            @pl.when(own)
            def _():
                rr[part, z] = rs[part, k]

            @pl.when(jnp.logical_not(own))
            def _():
                remote(
                    rs.at[part, k], rr.at[part, z], r_send.at[part, k], r_recv.at[part, z],
                    (d, zz * NX + xx, t),
                ).start()

        loop(0, 8, one)

    def outer(part):
        m_arrived(part, 1)

        def one(n):
            rows = pl.ds(pl.multiple_of(n * 128, 128), 128)
            if part == 0:
                out = dot(xt[1, rows, :], mm[0, :, :, :, 0:128].reshape(PLANE * 128, 128))
                gq = dot(xt[0, rows, :], mm[0, :, :, :, 128:256].reshape(PLANE * 128, 128))
                val = jnp.concatenate([out, gq], axis=1)
            else:
                val = dot(xt[0, rows, :], mm[1].reshape(PLANE * 128, 256))
            rs[part, pl.ds(2 * n, 2)] = val.astype(BF16).reshape(2, 64, 256)

        loop(0, 4, one)
        reduce_out(part)

    outer(0)
    outer(1)

    source = lax.div(z, 4)

    def r_arrived(part):
        def one(zz):
            @pl.when(jnp.logical_not((source == side) & (zz == z)))
            def _():
                arrived(rr.at[part, zz], r_recv.at[part, zz])
        loop(0, NZ, one)

    arrived(rssq, sib_recv.at[3])
    rssq[...] = lax.rsqrt(ssq[...] + rssq[...] + 1e-06) * (1.0 / 128.0)
    for part, places in ((0, (3, 0)), (1, (1, 2))):
        r_arrived(part)
        total = jnp.sum(rr[part].astype(F32), axis=0)
        for n, m in enumerate(places):
            proj_out[:, m, :] = total[:, n * 128:(n + 1) * 128] * rssq[m:m + 1, low_half]

    def kv_left(s):
        for h in range(2):
            @pl.when((z >= s) & (s <= 3) & (z <= NZ - 2))
            def _():
                left(kvg.at[0, h], kv_send_z.at[s, h])

            @pl.when((z >= s) & ((xh == 0) | (s >= 1)))
            def _():
                left(kvg.at[0, h], kv_send_x.at[s, h])

            @pl.when((z >= s) & (s >= 1))
            def _():
                left(dsend.at[0, h], t_send.at[s, h])

        @pl.when((z + xh >= s + 1) & ((xh == 1) | (s <= 3)))
        def _():
            left(dsend.at[0], x_send.at[s])

    loop(0, 5, kv_left)

    @pl.when((xh == 1) & (z >= 4) & (z <= NZ - 2))
    def _():
        for h in range(2):
            left(kvg.at[0, h], kv_send_9.at[h])

    @pl.when((xh == 0) & (z >= 5))
    def _():
        left(dsend.at[0], ext_send.at[0])

    for copy in bx_copies + by_copies:
        copy.wait_send()
    for k in range(4):
        for copy in ring_copies(k):
            copy.wait_send()
    for n in range(2):
        for p in range(NZ):
            left(bas.at[0, 0, LOW], yf_send.at[n, p])
    for part in range(2):
        for n in range(2):
            for stage in range(2):
                loop(1, 4, lambda k: m_parts(part, n, stage, k)[0]().wait_send())

    def plane_left(k):
        left(xr.at[0, 0], a_send.at[k])

    loop(1, PLANE, plane_left)
    for copy in (hand_over, give_a, give_b, give_s):
        copy.wait_send()

    def reduce_left(k):
        zz, xx = piece_device(k)

        @pl.when(jnp.logical_not((zz == z) & (xx == xh)))
        def _():
            left(rs.at[0, 0], r_send.at[0, k])
            left(rs.at[1, 0], r_send.at[1, k])

    loop(0, 8, reduce_left)


def on_device(*args):
    dma = pltpu.SemaphoreType.DMA
    vmem = pltpu.VMEM
    scratch = [
        vmem((128, 2048), BF16), vmem((128, 2048), BF16),
        vmem((2, 1024, 128), BF16), vmem((2, 1024, 128), BF16),
        vmem((2, 128, 1024), BF16), vmem((2, 128, 1024), BF16),
        vmem((LONGEST, 2, 128, 256), BF16),
        vmem((LONGEST, 2, 128, 1024), F32),
        vmem((2, 1, 1024), F32), vmem((2, 1, 1024), F32), vmem((2, 1, 1024), F32),
        vmem((2, 128, 1024), F32), vmem((2, 128, 1024), F32),
        vmem((LONGEST, 2, 128, 256), BF16), vmem((5, 2, 128, 256), F32),
        vmem((5, 2, 128, 256), BF16), vmem((4, 2, 128, 256), BF16),
        vmem((2, 128, 256), BF16),
        vmem((2, 2, 288, 256), BF16), vmem((2, 288, 256), BF16), vmem((4, 288, 256), BF16),
        vmem((2, NZ, 288, 256), BF16),
        vmem((2, PLANE, 128, 512), BF16), vmem((2, 512, 2048), BF16),
        vmem((2, 2, 128, 256), F32), vmem((2, 2, 128, 128), BF16), vmem((2, 2, 128, 128), BF16),
        vmem((2, 4, 4, 128, 256), BF16),
        vmem((2, 8, 64, 256), BF16), vmem((2, 8, 64, 256), BF16),
        vmem((4, 256), F32), vmem((4, 256), F32),
        dma((8,)),
        dma((10, 2)), dma((4, 2)), dma((5, 2)), dma((2,)),
        dma((5,)), dma((5,)), dma((5, 2)), dma((4, 2)), dma((1,)), dma((1,)),
        dma((2, 2)), dma((2, 2)), dma((4,)), dma((4,)), dma((2, 4)), dma((2, 4)), dma((2, NZ)), dma((2, NZ)),
        dma((PLANE,)), dma((PLANE,)), dma((4,)), dma((4,)),
        dma((2, 2, 2, 4)), dma((2, 2, 2, 4)), dma((2, 8)), dma((2, 8)),
    ]
    hbm = pl.BlockSpec(memory_space=pl.ANY)
    smem = pl.BlockSpec(memory_space=pltpu.SMEM)
    return pl.pallas_call(
        kernel,
        out_shape=(
            pltpu.VMEM((1, 128, 2048), BF16),
            pltpu.VMEM((1, 128, 2048), BF16),
            pltpu.VMEM((2, 1, 128, 256), BF16),
            pltpu.VMEM((64, 4, 128), F32),
        ),
        in_specs=[hbm] * 5 + [smem] + [hbm] * 2 + [smem],
        out_specs=(pl.BlockSpec(memory_space=pltpu.VMEM),) * 4,
        scratch_shapes=scratch,
        compiler_params=pltpu.CompilerParams(
            collective_id=0, has_side_effects=True, vmem_limit_bytes=60 * 1024 * 1024
        ),
        cost_estimate=pl.CostEstimate(flops=7_000_000_000, bytes_accessed=12_000_000, transcendentals=3_000_000),
    )(*args)


def solution(mesh):
    return jax.shard_map(
        on_device,
        mesh=mesh,
        in_specs=(
            P("dp", "ctx", None),
            P("dp", "ctx", "tp"),
            P(None, "dp", "ctx", "tp"),
            P("dp", "ctx", "tp"),
            P("dp", "ctx", None),
            P("dp", None),
            P(None, "dp", None, None),
            P(None, "dp", None, None),
            P(),
        ),
        out_specs=(
            P("dp", "ctx", "tp"),
            P("dp", "ctx", "tp"),
            P(None, "dp", "ctx", "tp"),
            P(("dp", "ctx"), None, "tp"),
        ),
        check_vma=False,
    )
```

time: 149 us -> 110 us (0.74); the launches traced: 146 us -> 109 us
  Pallas kernels: 140 us -> 105 us
  local copies, waits for them, and re-layouts: 5.12 us -> 2.9 us
    pallas_call x1, Pallas kernels: 140 us -> 105 us  [on_device(): pl.pallas_call(kernel, out_shape=(pltpu.VMEM((1, 128, 2048), BF16), pltpu...]
    unnamed x8 -> x4, local copies, waits for them, and re-layouts: 5.12 us -> 2.9 us
where the time goes in v2:
time: 110 us; the launch traced here: 109 us
  Pallas kernels  105 us (95%)
  local copies, waits for them, and re-layouts  2.9 us (3%)
    pallas_call x1, Pallas kernels, on_device(): pl.pallas_call(kernel, out_shape=(pltpu.VMEM((1, 128, 2048), BF16), pltpu...  105 us
    unnamed x4, local copies, waits for them, and re-layouts  2.9 us

profile of v2, /device:TPU:6, one launch (start us, length us, event | category | flops | bytes accessed | tf_op | source)
XLA Modules:
  0.0 108.8 jit_solution(10593577228269905089)
XLA Ops:
  0.6 105.3 %shard_map.120 = (bf16[1,128,2048]{2,1,0:T(8,128)(2,1)S(1)}, bf16[1,128,2048]{2,1,0:T(8,128)(2,1)S(1)}, bf16[2,1,128,256]{3,2,1,0:T(8,128)(2,1)S(1)}, f32[64,4,128]{2,1,0:T(4,128)S(1)}) custom-call(bf16[1,128,8192]{2,1,0:T(8,128)(2,1)} %x_ref.1, bf16[1,128,2048]{2,1,0:T(8,128)(2,1)} %q_ref.1, bf16[2,1,128,256]{3,2,1,0:T(8,128)(2,1)} %kv_ref.1, ...), custom_call_target="tpu_custom_call" | custom-call | flops 7000000000 | bytes 12000000 | tf_op jit(solution)/shard_map/pallas_call | solution.py:682
  105.9 0.8 copy.17
  106.7 0.7 copy.19
  107.4 0.7 copy.20
  108.0 0.8 copy.18

commit v3 on v2

--- a/solution.py
+++ b/solution.py
@@ -19,7 +19,6 @@
 NX = 2
 NY = 4
 NZ = 8
-PLANE = NX * NX * NY
 
 
 def dot(a, b, dims=((1,), (0,))):
@@ -29,23 +28,21 @@
 def kernel(
     x_ref, q_ref, kv_ref, do_ref, gl_ref, docs_ref, wide_ref, narrow_ref, owner_ref,
     att_out, gq_out, gkv_out, proj_out,
-    qf, dof, qs, dos, qt, dot_, kvg, w, mx, den, delta, ot, dqt,
+    qf, dof, qs, dos, qt, dot_, kvg, w, mx, at, den, delta, ot, otl, dqt,
     dsend, dacc, xrecv, tin, ext,
-    bx, pk, by, bas, xr, xt, pm, sx, rx, mm, rs, rr, ssq, rssq,
+    bx, pk, by, bas, relay, xr, xt, pm, sx, rx, mm, rs, rr, rs2, rr2, ssq, rssq,
     load_sem,
     kv_recv, kv_send_z, kv_send_x, kv_send_9,
     x_send, x_recv, t_send, t_recv, ext_send, ext_recv,
     bx_send, bx_recv, by_send, by_recv, ring_send, ring_recv, yf_send, yf_recv,
-    a_send, a_recv, sib_send, sib_recv, m_send, m_recv, r_send, r_recv,
+    a_send, a_recv, relay_send, relay_recv, sib_send, sib_recv, m_send, m_recv, r_send, r_recv, z_send, z_recv,
 ):
     d = lax.axis_index("dp")
     c = lax.axis_index("ctx")
     t = lax.axis_index("tp")
     y, xl = lax.div(d, NX), lax.rem(d, NX)
     z, xh = lax.div(c, NX), lax.rem(c, NX)
-    plane = d * NX + xh
-    odd, odd_z = lax.rem(y, 2), lax.rem(z, 2)
-    side = xh + odd_z * (1 - 2 * xh)
+    odd = lax.rem(y, 2)
     partner = (d, c + 1 - 2 * xh, t)
     above = (d, c + NX, t)
     below = (d, c - NX, t)
@@ -86,66 +83,66 @@
     for half in range(2):
         for n, (source, rows) in enumerate(zip(mine_of(half), (pl.ds(0, 256), pl.ds(256, 32)))):
             b_loads.append(local(source, bx.at[half, xl, rows], load_sem.at[3 + 2 * half + n]))
+    barrier = pltpu.get_barrier_semaphore()
+
+    def greet(device):
+        pl.semaphore_signal(barrier, inc=1, device_id=device, device_id_type=MESH)
+
+    def y_device(k):
+        return (lax.rem(y + k, NY) * NX + xl, c, t)
+
+    def dp_device(k):
+        other = lax.rem(d + k, NX * NY)
+        return other, (other, c, t)
+
+    loop(1, NX * NY, lambda k: greet(dp_device(k)[1]))
+    greet(partner)
+    greet((d + 1 - 2 * xl, c + 1 - 2 * xh, t))
+
+    place = xl * NY + y
+
+    def greet_column(k):
+        zz = lax.rem(z + k, NZ)
+        greet((d, zz * NX, t))
+        greet((d, zz * NX + 1, t))
+
+    loop(1, NZ, greet_column)
+    greet(sibling)
     kv_load.start()
     q_load.start()
     do_load.start()
     for copy in b_loads:
         copy.start()
 
-    barrier = pltpu.get_barrier_semaphore()
-
-    def greet(device):
-        pl.semaphore_signal(barrier, inc=1, device_id=device, device_id_type=MESH)
-
-    def plane_device(k):
-        other = lax.rem(plane + k, PLANE)
-        return other, (lax.div(other, NX), z * NX + lax.rem(other, NX), t)
-
-    loop(1, PLANE, lambda k: greet(plane_device(k)[1]))
-
-    def greet_column(k):
-        zz = lax.rem(z + k, NZ)
-        greet((d, zz * NX, t))
-        greet((d, zz * NX + 1, t))
-
-    loop(1, NZ, greet_column)
-    greet(sibling)
-
-    def split_heads(h):
-        g, i = lax.div(h, 8), lax.rem(h, 8)
-        columns = pl.ds(pl.multiple_of(h * HEAD, HEAD), HEAD)
-        rows = pl.ds(pl.multiple_of(i * HEAD, HEAD), HEAD)
-        tile = qf[:, columns]
-        qs[g, rows, :] = tile
-        qt[g, :, rows] = tile.T
-        tile = dof[:, columns]
-        dos[g, rows, :] = tile
-        dot_[g, :, rows] = tile.T
-
-    q_load.wait()
-    do_load.wait()
-    loop(0, 16, split_heads)
-    kv_load.wait()
-
-    def score(j, diagonal=False):
+    def attend(j, diagonal=False):
         if not diagonal:
             same = docs_ref[0, c] == docs_ref[0, c - j]
             bias = jnp.where(same, 0.0, NEG).astype(F32)
         for g in range(2):
-            key = kvg[j, 0, :, g * HEAD:(g + 1) * HEAD]
-            s = dot(key, qt[g]) * INV_ROOT
+            columns = slice(g * HEAD, (g + 1) * HEAD)
+            s = dot(kvg[j, 0, :, columns], qt[g]) * INV_ROOT
             if diagonal:
                 rows = lax.broadcasted_iota(jnp.int32, s.shape, 0)
                 lanes = lax.broadcasted_iota(jnp.int32, s.shape, 1) & (BLOCK - 1)
                 s = jnp.where(rows <= lanes, s, NEG)
-                mx[g] = jnp.max(s, axis=0, keepdims=True)
+                top = jnp.max(s, axis=0, keepdims=True)
             else:
                 s = s + bias
-                mx[g] = jnp.maximum(mx[g], jnp.max(s, axis=0, keepdims=True))
-            w[j, g] = s
-
-    score(0, True)
-    pl.semaphore_wait(barrier, (PLANE - 1) + 2 * (NZ - 1) + 1)
+                top = jnp.maximum(mx[g], jnp.max(s, axis=0, keepdims=True))
+            p = jnp.exp(s - top)
+            w[j, g] = p
+            at[j, g] = top
+            term = dot(kvg[j, 1, :, columns], p.astype(BF16), ((0,), (0,)))
+            total = jnp.sum(p, axis=0, keepdims=True)
+            if not diagonal:
+                factor = jnp.exp(mx[g] - top)
+                term += ot[g] * factor
+                total += den[g] * factor
+            mx[g] = top
+            ot[g] = term
+            den[g] = total
+
+    pl.semaphore_wait(barrier, (NX * NY - 1) + 2 + 2 * (NZ - 1) + 1)
 
     def forward_kv(s, h):
         slot = 2 * s
@@ -169,6 +166,7 @@
         def _():
             to(9, kv_send_9.at[h], (d, c + 1, t))
 
+    kv_load.wait()
     forward_kv(0, 0)
     forward_kv(0, 1)
 
@@ -184,26 +182,54 @@
     for copy in bx_copies:
         copy.start()
 
-    def columns_of(p):
-        p = p + odd_z * (1 - 2 * lax.rem(p, 2))
-        return pl.ds(pl.multiple_of(p * 512, 512), 512)
-
     def send_inputs(steps):
         for core, source in enumerate((x_ref, gl_ref)):
             @pl.when(t == core)
             def _():
-                for k in steps:
-                    other, device = plane_device(k)
-                    remote(
-                        source.at[0, :, columns_of(other)], xr.at[core, plane], a_send.at[k], a_recv.at[plane], device
-                    ).start()
-                if 4 in steps:
-                    local(source.at[0, :, columns_of(plane)], xr.at[core, plane], load_sem.at[7]).start()
-
-    send_inputs((4, 8, 12))
-
-    def y_device(k):
-        return (lax.rem(y + k, NY) * NX + xl, c, t)
+                for dy, dx in steps:
+                    row = lax.rem(y + dy, NY)
+                    other = row * NX + side(dx)
+                    part = source.at[0, :, pl.ds(pl.multiple_of(other * 1024, 1024), 1024)]
+                    send = a_send.at[dy * NX + dx]
+                    if dy == dx == 0:
+                        local(part, xr.at[core, place], load_sem.at[7]).start()
+                    elif dy == 0:
+                        remote(part, xr.at[core, place], send, a_recv.at[place], x_pair).start()
+                    elif dx == 0:
+                        remote(part, xr.at[core, place], send, a_recv.at[place], y_device(dy)).start()
+                    else:
+                        remote(part, relay.at[y], send, relay_recv.at[y], y_device(dy)).start()
+
+    def relay_copy(k):
+        row = lax.rem(y + k, NY)
+        slot = xl * NY + row
+        return remote(relay.at[row], xr.at[t, slot], relay_send.at[row], a_recv.at[slot], x_pair)
+
+    def relay_on(k):
+        row = lax.rem(y + k, NY)
+        arrived(relay.at[row], relay_recv.at[row])
+        relay_copy(k).start()
+
+    def side(dx):
+        return xl if dx == 0 else 1 - xl
+
+    send_inputs(((1, 0), (3, 0), (0, 0), (1, 1), (3, 1)))
+
+    def split_heads(h):
+        g, i = lax.div(h, 8), lax.rem(h, 8)
+        columns = pl.ds(pl.multiple_of(h * HEAD, HEAD), HEAD)
+        rows = pl.ds(pl.multiple_of(i * HEAD, HEAD), HEAD)
+        tile = qf[:, columns]
+        qs[g, rows, :] = tile
+        qt[g, :, rows] = tile.T
+        tile = dof[:, columns]
+        dos[g, rows, :] = tile
+        dot_[g, :, rows] = tile.T
+
+    q_load.wait()
+    do_load.wait()
+    loop(0, 16, split_heads)
+    attend(0, True)
 
     by_copies = [
         remote(pk.at[odd if k == 2 else 1 - odd], by.at[y], by_send.at[k], by_recv.at[y], y_device(k))
@@ -271,16 +297,17 @@
 
     def odd_slot(j):
         arrived(kvg.at[j, 0], kv_recv.at[j, 0])
-        score(j)
+        arrived(kvg.at[j, 1], kv_recv.at[j, 1])
+        attend(j)
 
     def forward_step(s):
         @pl.when(z >= s)
         def _():
             arrived(kvg.at[2 * s, 0], kv_recv.at[2 * s, 0])
             forward_kv(s, 0)
-            score(2 * s)
             arrived(kvg.at[2 * s, 1], kv_recv.at[2 * s, 1])
             forward_kv(s, 1)
+            attend(2 * s)
 
         @pl.when((s >= 2) & (z + xh >= s - 1))
         def _():
@@ -301,50 +328,28 @@
 
     loop(4, 6, last_slots)
 
-    def odd_values(s):
-        @pl.when(z + xh >= s)
-        def _():
-            arrived(kvg.at[2 * s - 1, 1], kv_recv.at[2 * s - 1, 1])
-
-    loop(1, 6, odd_values)
-    ring_step(1)
-
-    send_inputs((1, 2, 3, 5, 6, 7))
-
-    den[...] = jnp.zeros_like(den)
-    ot[...] = jnp.zeros_like(ot)
+    send_inputs(((0, 1), (2, 0), (2, 1)))
+
     dqt[...] = jnp.zeros_like(dqt)
-
-    def weigh(j):
-        for g in range(2):
-            value = kvg[j, 1, :, g * HEAD:(g + 1) * HEAD]
-            p = jnp.exp(w[j, g] - mx[g])
-            w[j, g] = p
-            den[g] += jnp.sum(p, axis=0, keepdims=True)
-            ot[g] += dot(value, p.astype(BF16), ((0,), (0,)))
-
-    loop(0, jnp.minimum(c, LONGEST - 1) + 1, weigh)
     for g in range(2):
         den[g] = 1.0 / den[g]
-
-    def finish_heads(h):
-        g, i = lax.div(h, 8), lax.rem(h, 8)
-        columns = pl.ds(pl.multiple_of(h * HEAD, HEAD), HEAD)
-        rows = pl.ds(pl.multiple_of(i * HEAD, HEAD), HEAD)
-        low = (ot[g, :, rows] * den[g, :, rows]).astype(BF16)
-        wide = low.astype(F32) * dot_[g, :, rows].astype(F32)
-        delta[g, :, rows] = jnp.sum(wide, axis=0, keepdims=True)
-        att_out[0, :, columns] = low.T
-
-    loop(0, 16, finish_heads)
-    ring_step(2)
+        low = (ot[g] * den[g]).astype(BF16)
+        otl[g] = low
+        delta[g] = jnp.sum(low.astype(F32) * dot_[g].astype(F32), axis=0, keepdims=True)
+
+    def scale(j):
+        for g in range(2):
+            at[j, g] = jnp.exp(at[j, g] - mx[g]) * den[g]
+
+    loop(0, jnp.minimum(c, LONGEST - 1) + 1, scale)
+    ring_step(1)
 
     def backward(j, store):
         for g in range(2):
             columns = slice(g * HEAD, (g + 1) * HEAD)
             key = kvg[j, 0, :, columns]
             value = kvg[j, 1, :, columns]
-            p = w[j, g] * den[g]
+            p = w[j, g] * at[j, g]
             ds = (p * (dot(value, dot_[g]) - delta[g])).astype(BF16)
             dqt[g] += dot(key, ds, ((0,), (0,)))
             store(0, columns, dot(ds, qs[g]) * INV_ROOT)
@@ -405,30 +410,62 @@
 
             backward(2 * s, store)
 
-        @pl.when(i >= 3)
-        def _():
-            chain(s + 3)
-
         @pl.when(i == 1)
         def _():
+            ring_step(2)
+
+        @pl.when(i == 2)
+        def _():
+            relay_on(1)
+
+        @pl.when(i == 3)
+        def _():
             ring_step(3)
 
-        @pl.when(i == 3)
-        def _():
-            ring_step(4)
-
     loop(0, 5, backward_step)
-    chain(2)
-    send_inputs((9, 10, 11, 13, 14, 15))
+    relay_on(3)
+    ring_step(4)
+    chain(4)
+    relay_on(2)
 
     def finish_grads(h):
         g, i = lax.div(h, 8), lax.rem(h, 8)
         columns = pl.ds(pl.multiple_of(h * HEAD, HEAD), HEAD)
         rows = pl.ds(pl.multiple_of(i * HEAD, HEAD), HEAD)
         gq_out[0, :, columns] = (dqt[g, :, rows] * INV_ROOT).astype(BF16).T
+        att_out[0, :, columns] = otl[g, :, rows].T
 
     loop(0, 16, finish_grads)
-    chain(1)
+    chain(3)
+    hand_overs = [
+        remote(ref, ref, sib_send.at[n], sib_recv.at[n], sibling)
+        for n, ref in ((0, xr.at[t, pl.ds(xl * NY, NY)]), (4, xr.at[t, pl.ds((1 - xl) * NY, NY)]))
+    ]
+
+    def inputs_arrived(dx):
+        for k in range(NY):
+            at_y = side(dx) * NY + lax.rem(y + k, NY)
+            if dx == 0 and k == 0:
+                local(xr.at[t, place], xr.at[t, place], load_sem.at[7]).wait()
+            else:
+                arrived(xr.at[t, at_y], a_recv.at[at_y])
+        hand_overs[dx].start()
+
+    def other_arrived(dx):
+        arrived(xr.at[1 - t, pl.ds(side(dx) * NY, NY)], sib_recv.at[4 * dx])
+
+    def turn(a, dx):
+        def one(n):
+            other, group = side(dx) * NY + lax.div(n, 2), lax.rem(n, 2)
+            tokens = pl.ds(pl.multiple_of(other * 128, 128), 128)
+            for m in range(4):
+                rows = pl.ds(pl.multiple_of(group * 512 + m * 128, 128), 128)
+                xt[a, rows, tokens] = xr[a, other, :, rows].T
+        loop(0, NY * 2, one)
+
+    inputs_arrived(0)
+    chain(2)
+    turn(t, 0)
 
     for n in range(2):
         for p in range(NZ):
@@ -445,45 +482,24 @@
         copy.start()
         return copy
 
-    quad = xl * NX + xh
-
-    def m_parts(part, n, stage, k):
-        if n == stage:
-            other = lax.rem(quad + k, 4)
-            device = (y * NX + lax.div(other, NX), z * NX + lax.rem(other, NX), t)
-            mine, theirs = quad, other
-        else:
-            other = lax.rem(y + k, NY)
-            device = (other * NX + xl, c, t)
-            mine, theirs = y, other
-        lanes = pl.ds(n * 128, 128)
-
-        def ref(at):
-            if stage == 0:
-                return mm.at[part, y, at, :, lanes] if n == 0 else mm.at[part, at, quad, :, lanes]
-            return mm.at[part, at, :, :, lanes] if n == 0 else mm.at[part, :, at, :, lanes]
-
-        return (
-            lambda: remote(
-                ref(mine), ref(mine), m_send.at[part, n, stage, k], m_recv.at[part, n, stage, mine], device
-            ),
-            (ref(theirs), m_recv.at[part, n, stage, theirs]),
-        )
-
-    def m_start(part, stage):
-        for n in range(2):
-            loop(1, 4, lambda k: m_parts(part, n, stage, k)[0]().start())
-
-    def m_arrived(part, stage):
-        for n in range(2):
-            loop(1, 4, lambda k: arrived(*m_parts(part, n, stage, k)[1]))
+    def m_copy(part, k):
+        ref = mm.at[part, place]
+        return remote(ref, ref, m_send.at[part, k], m_recv.at[part, place], dp_device(k)[1])
+
+    def m_arrived(part):
+        def one(k):
+            other, _ = dp_device(k)
+            slot = lax.rem(other, NX) * NY + lax.div(other, NX)
+            arrived(mm.at[part, slot], m_recv.at[part, slot])
+
+        loop(1, NX * NY, one)
 
     def spread(part):
         arrived(rx.at[part], sib_recv.at[1 + part])
         for n in range(2):
             share = pm[part, n, :, low_half] + rx[part, n].astype(F32)
-            mm[part, y, quad, :, n * 128:(n + 1) * 128] = share.astype(BF16)
-        m_start(part, 0)
+            mm[part, place, :, n * 128:(n + 1) * 128] = share.astype(BF16)
+        loop(1, NX * NY, lambda k: m_copy(part, k).start())
 
     def wide_basis(half):
         return bas[half, :, 0:256, :].reshape(NZ * 256, 256)
@@ -492,14 +508,74 @@
         return bas[half, :, 256:288, :].reshape(NZ * 32, 256)
 
     give_a = give(0, ((att_out[0], wide_basis(1)), (gq_out[0], wide_basis(0))))
+    chain(1)
     spread(0)
+    other_arrived(0)
+    turn(1 - t, 0)
+
     chain(0)
     for h in range(2):
         gkv_out[h, 0] = dacc[0, h].astype(BF16)
     give_b = give(1, ((gkv_out[0, 0], narrow_basis(0)), (gkv_out[1, 0], narrow_basis(1))))
     spread(1)
-    m_arrived(0, 0)
-    m_start(0, 1)
+
+    def x_copy(part):
+        return remote(rs.at[part, 1 - xh], rr.at[part], r_send.at[part], r_recv.at[part], partner)
+
+    def outer(part):
+        tokens = NX * NY * 128
+
+        def one(n):
+            rows = pl.ds(pl.multiple_of(n * 256, 256), 256)
+            if part == 0:
+                out = dot(xt[1, rows, :], mm[0, :, :, 0:128].reshape(tokens, 128))
+                gq = dot(xt[0, rows, :], mm[0, :, :, 128:256].reshape(tokens, 128))
+                val = jnp.concatenate([out, gq], axis=1).astype(BF16)
+            else:
+                val = dot(xt[0, rows, :], mm[1].reshape(tokens, 256)).astype(BF16)
+            for m in range(2):
+                rs[part, 0, 2 * n + m] = val[m * 128:m * 128 + 64]
+                rs[part, 1, 2 * n + m] = val[m * 128 + 64:m * 128 + 128]
+
+        loop(0, NZ // 2, one)
+        x_copy(part).start()
+
+    def z_copy(part, k):
+        zz = lax.rem(z + k, NZ)
+        return remote(
+            rs2.at[part, zz], rr2.at[part, z], z_send.at[part, k], z_recv.at[part, z], (d, zz * NX + xh, t)
+        )
+
+    def over_x(part):
+        arrived(rr.at[part], r_recv.at[part])
+
+        def one(zz):
+            total = rs[part, xh, zz].astype(F32) + rr[part, zz].astype(F32)
+            rs2[part, zz] = total.astype(BF16)
+
+        loop(0, NZ, one)
+        loop(1, NZ, lambda k: z_copy(part, k).start())
+
+    def over_z(part, places):
+        def one(k):
+            zz = lax.rem(z + k, NZ)
+            arrived(rr2.at[part, zz], z_recv.at[part, zz])
+
+        loop(1, NZ, one)
+        total = rs2[part, z].astype(F32)
+        for k in range(1, NZ):
+            total += rr2[part, lax.rem(z + k, NZ)].astype(F32)
+        for n, m in enumerate(places):
+            proj_out[:, m, :] = total[:, n * 128:(n + 1) * 128] * rssq[m:m + 1, low_half]
+
+    inputs_arrived(1)
+    turn(t, 1)
+    other_arrived(1)
+    turn(1 - t, 1)
+    m_arrived(0)
+    outer(0)
+    m_arrived(1)
+    outer(1)
     for m, value in enumerate((wide_basis(0), narrow_basis(0), narrow_basis(1), wide_basis(1))):
         wide = value.astype(F32)
         ssq[m:m + 1, :] = jnp.sum(wide * wide, axis=0, keepdims=True)
@@ -507,87 +583,12 @@
     give_s.start()
 
 
-    local(xr.at[t, plane], xr.at[t, plane], load_sem.at[7]).wait()
-
-    def a_arrived(k):
-        other = lax.rem(plane + k, PLANE)
-        arrived(xr.at[t, other], a_recv.at[other])
-
-    loop(1, PLANE, a_arrived)
-    hand_over = remote(xr.at[t], xr.at[t], sib_send.at[0], sib_recv.at[0], sibling)
-    hand_over.start()
-
-    def turn(a):
-        def one(p):
-            for n in range(4):
-                xt[a, n * 128:(n + 1) * 128, pl.ds(pl.multiple_of(p * 128, 128), 128)] = (
-                    xr[a, p, :, n * 128:(n + 1) * 128].T
-                )
-        loop(0, PLANE, one)
-
-    turn(t)
-    m_arrived(1, 0)
-    m_start(1, 1)
-    arrived(xr.at[1 - t], sib_recv.at[0])
-    turn(1 - t)
-
-    def piece_device(k):
-        zz = side * 4 + lax.div(k, 2)
-        return zz, lax.rem(k, 2)
-
-    def reduce_out(part):
-        def one(k):
-            zz, xx = piece_device(k)
-            own = (zz == z) & (xx == xh)
-
-            @pl.when(own)
-            def _():
-                rr[part, z] = rs[part, k]
-
-            @pl.when(jnp.logical_not(own))
-            def _():
-                remote(
-                    rs.at[part, k], rr.at[part, z], r_send.at[part, k], r_recv.at[part, z],
-                    (d, zz * NX + xx, t),
-                ).start()
-
-        loop(0, 8, one)
-
-    def outer(part):
-        m_arrived(part, 1)
-
-        def one(n):
-            rows = pl.ds(pl.multiple_of(n * 128, 128), 128)
-            if part == 0:
-                out = dot(xt[1, rows, :], mm[0, :, :, :, 0:128].reshape(PLANE * 128, 128))
-                gq = dot(xt[0, rows, :], mm[0, :, :, :, 128:256].reshape(PLANE * 128, 128))
-                val = jnp.concatenate([out, gq], axis=1)
-            else:
-                val = dot(xt[0, rows, :], mm[1].reshape(PLANE * 128, 256))
-            rs[part, pl.ds(2 * n, 2)] = val.astype(BF16).reshape(2, 64, 256)
-
-        loop(0, 4, one)
-        reduce_out(part)
-
-    outer(0)
-    outer(1)
-
-    source = lax.div(z, 4)
-
-    def r_arrived(part):
-        def one(zz):
-            @pl.when(jnp.logical_not((source == side) & (zz == z)))
-            def _():
-                arrived(rr.at[part, zz], r_recv.at[part, zz])
-        loop(0, NZ, one)
-
+    over_x(0)
     arrived(rssq, sib_recv.at[3])
     rssq[...] = lax.rsqrt(ssq[...] + rssq[...] + 1e-06) * (1.0 / 128.0)
-    for part, places in ((0, (3, 0)), (1, (1, 2))):
-        r_arrived(part)
-        total = jnp.sum(rr[part].astype(F32), axis=0)
-        for n, m in enumerate(places):
-            proj_out[:, m, :] = total[:, n * 128:(n + 1) * 128] * rssq[m:m + 1, low_half]
+    over_x(1)
+    over_z(0, (3, 0))
+    over_z(1, (1, 2))
 
     def kv_left(s):
         for h in range(2):
@@ -626,27 +627,20 @@
     for n in range(2):
         for p in range(NZ):
             left(bas.at[0, 0, LOW], yf_send.at[n, p])
+    def dp_left(k):
+        left(xr.at[0, 0], a_send.at[k])
+        for part in range(2):
+            m_copy(part, k).wait_send()
+
+    loop(1, NX * NY, dp_left)
     for part in range(2):
-        for n in range(2):
-            for stage in range(2):
-                loop(1, 4, lambda k: m_parts(part, n, stage, k)[0]().wait_send())
-
-    def plane_left(k):
-        left(xr.at[0, 0], a_send.at[k])
-
-    loop(1, PLANE, plane_left)
-    for copy in (hand_over, give_a, give_b, give_s):
+        x_copy(part).wait_send()
+    for k in range(1, NY):
+        relay_copy(k).wait_send()
+    for part in range(2):
+        loop(1, NZ, lambda k: z_copy(part, k).wait_send())
+    for copy in (*hand_overs, give_a, give_b, give_s):
         copy.wait_send()
-
-    def reduce_left(k):
-        zz, xx = piece_device(k)
-
-        @pl.when(jnp.logical_not((zz == z) & (xx == xh)))
-        def _():
-            left(rs.at[0, 0], r_send.at[0, k])
-            left(rs.at[1, 0], r_send.at[1, k])
-
-    loop(0, 8, reduce_left)
 
 
 def on_device(*args):
@@ -658,24 +652,25 @@
         vmem((2, 128, 1024), BF16), vmem((2, 128, 1024), BF16),
         vmem((LONGEST, 2, 128, 256), BF16),
         vmem((LONGEST, 2, 128, 1024), F32),
-        vmem((2, 1, 1024), F32), vmem((2, 1, 1024), F32), vmem((2, 1, 1024), F32),
-        vmem((2, 128, 1024), F32), vmem((2, 128, 1024), F32),
+        vmem((2, 1, 1024), F32), vmem((LONGEST, 2, 1, 1024), F32), vmem((2, 1, 1024), F32), vmem((2, 1, 1024), F32),
+        vmem((2, 128, 1024), F32), vmem((2, 128, 1024), BF16), vmem((2, 128, 1024), F32),
         vmem((LONGEST, 2, 128, 256), BF16), vmem((5, 2, 128, 256), F32),
         vmem((5, 2, 128, 256), BF16), vmem((4, 2, 128, 256), BF16),
         vmem((2, 128, 256), BF16),
         vmem((2, 2, 288, 256), BF16), vmem((2, 288, 256), BF16), vmem((4, 288, 256), BF16),
         vmem((2, NZ, 288, 256), BF16),
-        vmem((2, PLANE, 128, 512), BF16), vmem((2, 512, 2048), BF16),
+        vmem((NY, 128, 1024), BF16), vmem((2, NX * NY, 128, 1024), BF16), vmem((2, 1024, NX * NY * 128), BF16),
         vmem((2, 2, 128, 256), F32), vmem((2, 2, 128, 128), BF16), vmem((2, 2, 128, 128), BF16),
-        vmem((2, 4, 4, 128, 256), BF16),
-        vmem((2, 8, 64, 256), BF16), vmem((2, 8, 64, 256), BF16),
+        vmem((2, NX * NY, 128, 256), BF16),
+        vmem((2, NX, NZ, 64, 256), BF16), vmem((2, NZ, 64, 256), BF16),
+        vmem((2, NZ, 64, 256), BF16), vmem((2, NZ, 64, 256), BF16),
         vmem((4, 256), F32), vmem((4, 256), F32),
         dma((8,)),
         dma((10, 2)), dma((4, 2)), dma((5, 2)), dma((2,)),
         dma((5,)), dma((5,)), dma((5, 2)), dma((4, 2)), dma((1,)), dma((1,)),
         dma((2, 2)), dma((2, 2)), dma((4,)), dma((4,)), dma((2, 4)), dma((2, 4)), dma((2, NZ)), dma((2, NZ)),
-        dma((PLANE,)), dma((PLANE,)), dma((4,)), dma((4,)),
-        dma((2, 2, 2, 4)), dma((2, 2, 2, 4)), dma((2, 8)), dma((2, 8)),
+        dma((NX * NY,)), dma((NX * NY,)), dma((NY,)), dma((NY,)), dma((5,)), dma((5,)),
+        dma((2, NX * NY)), dma((2, NX * NY)), dma((2,)), dma((2,)), dma((2, NZ)), dma((2, NZ)),
     ]
     hbm = pl.BlockSpec(memory_space=pl.ANY)
     smem = pl.BlockSpec(memory_space=pltpu.SMEM)

time: 110 us -> 107 us (0.973)
  Pallas kernels: 105 us -> 103 us
    pallas_call x1, Pallas kernels: 105 us -> 103 us  [on_device(): pl.pallas_call(kernel, out_shape=(pltpu.VMEM((1, 128, 2048), BF16), pltpu...]
where the time goes in v3:
time: 107 us
  Pallas kernels  103 us (96%)
  local copies, waits for them, and re-layouts  2.9 us (3%)
    pallas_call x1, Pallas kernels, on_device(): pl.pallas_call(kernel, out_shape=(pltpu.VMEM((1, 128, 2048), BF16), pltpu...  103 us
    unnamed x4, local copies, waits for them, and re-layouts  2.9 us

profile of v3, /device:TPU:6, one launch (start us, length us, event | category | flops | bytes accessed | tf_op | source)
XLA Modules:
  0.0 106.9 jit_solution(4302405626680060422)
XLA Ops:
  0.6 103.3 %shard_map.120 = (bf16[1,128,2048]{2,1,0:T(8,128)(2,1)S(1)}, bf16[1,128,2048]{2,1,0:T(8,128)(2,1)S(1)}, bf16[2,1,128,256]{3,2,1,0:T(8,128)(2,1)S(1)}, f32[64,4,128]{2,1,0:T(4,128)S(1)}) custom-call(bf16[1,128,8192]{2,1,0:T(8,128)(2,1)} %x_ref.1, bf16[1,128,2048]{2,1,0:T(8,128)(2,1)} %q_ref.1, bf16[2,1,128,256]{3,2,1,0:T(8,128)(2,1)} %kv_ref.1, ...), custom_call_target="tpu_custom_call" | custom-call | flops 7000000000 | bytes 12000000 | tf_op jit(solution)/shard_map/pallas_call | solution.py:677
  104.0 0.8 copy.17
  104.7 0.7 copy.19
  105.4 0.7 copy.20
  106.1 0.8 copy.18

commit v4 on v3

--- a/solution.py
+++ b/solution.py
@@ -35,7 +35,7 @@
     kv_recv, kv_send_z, kv_send_x, kv_send_9,
     x_send, x_recv, t_send, t_recv, ext_send, ext_recv,
     bx_send, bx_recv, by_send, by_recv, ring_send, ring_recv, yf_send, yf_recv,
-    a_send, a_recv, relay_send, relay_recv, sib_send, sib_recv, m_send, m_recv, r_send, r_recv, z_send, z_recv,
+    a_send, a_recv, relay_send, relay_recv, piece_send, piece_recv, sib_send, sib_recv, m_send, m_recv, r_send, r_recv, z_send, z_recv,
 ):
     d = lax.axis_index("dp")
     c = lax.axis_index("ctx")
@@ -97,7 +97,8 @@
 
     loop(1, NX * NY, lambda k: greet(dp_device(k)[1]))
     greet(partner)
-    greet((d + 1 - 2 * xl, c + 1 - 2 * xh, t))
+    for k in range(NY):
+        greet((lax.rem(y + k, NY) * NX + 1 - xl, c + 1 - 2 * xh, t))
 
     place = xl * NY + y
 
@@ -142,7 +143,7 @@
             ot[g] = term
             den[g] = total
 
-    pl.semaphore_wait(barrier, (NX * NY - 1) + 2 + 2 * (NZ - 1) + 1)
+    pl.semaphore_wait(barrier, (NX * NY - 1) + 1 + NY + 2 * (NZ - 1) + 1)
 
     def forward_kv(s, h):
         slot = 2 * s
@@ -194,16 +195,18 @@
                     if dy == dx == 0:
                         local(part, xr.at[core, place], load_sem.at[7]).start()
                     elif dy == 0:
-                        remote(part, xr.at[core, place], send, a_recv.at[place], x_pair).start()
+                        remote(part, xr.at[core, place], send, a_recv.at[place], (x_pair, x_other)[core]).start()
                     elif dx == 0:
                         remote(part, xr.at[core, place], send, a_recv.at[place], y_device(dy)).start()
                     else:
                         remote(part, relay.at[y], send, relay_recv.at[y], y_device(dy)).start()
 
+    crossing = (d + 1 - 2 * xl, c + t * (1 - 2 * xh), t)
+
     def relay_copy(k):
         row = lax.rem(y + k, NY)
         slot = xl * NY + row
-        return remote(relay.at[row], xr.at[t, slot], relay_send.at[row], a_recv.at[slot], x_pair)
+        return remote(relay.at[row], xr.at[t, slot], relay_send.at[row], a_recv.at[slot], crossing)
 
     def relay_on(k):
         row = lax.rem(y + k, NY)
@@ -454,14 +457,18 @@
     def other_arrived(dx):
         arrived(xr.at[1 - t, pl.ds(side(dx) * NY, NY)], sib_recv.at[4 * dx])
 
-    def turn(a, dx):
-        def one(n):
-            other, group = side(dx) * NY + lax.div(n, 2), lax.rem(n, 2)
-            tokens = pl.ds(pl.multiple_of(other * 128, 128), 128)
+    def turn_piece(a, other):
+        tokens = pl.ds(pl.multiple_of(other * 128, 128), 128)
+
+        def one(group):
             for m in range(4):
                 rows = pl.ds(pl.multiple_of(group * 512 + m * 128, 128), 128)
                 xt[a, rows, tokens] = xr[a, other, :, rows].T
-        loop(0, NY * 2, one)
+
+        loop(0, 2, one)
+
+    def turn(a, dx):
+        loop(0, NY, lambda n: turn_piece(a, side(dx) * NY + n))
 
     inputs_arrived(0)
     chain(2)
@@ -482,24 +489,42 @@
         copy.start()
         return copy
 
-    def m_copy(part, k):
-        ref = mm.at[part, place]
-        return remote(ref, ref, m_send.at[part, k], m_recv.at[part, place], dp_device(k)[1])
+    def m_pieces(part):
+        pieces = []
+        for dx in range(NX):
+            for k in range(NY):
+                if dx == k == 0:
+                    continue
+                row = lax.rem(y + k, NY)
+                other = row * NX + side(dx)
+                slot = side(dx) * NY + row
+                if dx == 0 or part == 1:
+                    pieces.append((other, c, slot, dx * NY + k, 0, pl.ds(0, 256)))
+                else:
+                    pieces.append((other, c + 1 - 2 * xh, slot, dx * NY + k, 0, pl.ds(0, 128)))
+                    pieces.append((other, c, slot, dx * NY + k, 1, pl.ds(128, 128)))
+        return pieces
+
+    def m_copies(part):
+        copies = []
+        for other, column, _, at_send, n, lanes in m_pieces(part):
+            ref = mm.at[part, place, :, lanes]
+            copies.append(
+                remote(ref, ref, m_send.at[part, at_send, n], m_recv.at[part, place, n], (other, column, t))
+            )
+        return copies
 
     def m_arrived(part):
-        def one(k):
-            other, _ = dp_device(k)
-            slot = lax.rem(other, NX) * NY + lax.div(other, NX)
-            arrived(mm.at[part, slot], m_recv.at[part, slot])
-
-        loop(1, NX * NY, one)
+        for _, _, slot, _, n, lanes in m_pieces(part):
+            arrived(mm.at[part, slot, :, lanes], m_recv.at[part, slot, n])
 
     def spread(part):
         arrived(rx.at[part], sib_recv.at[1 + part])
         for n in range(2):
             share = pm[part, n, :, low_half] + rx[part, n].astype(F32)
             mm[part, place, :, n * 128:(n + 1) * 128] = share.astype(BF16)
-        loop(1, NX * NY, lambda k: m_copy(part, k).start())
+        for copy in m_copies(part):
+            copy.start()
 
     def wide_basis(half):
         return bas[half, :, 0:256, :].reshape(NZ * 256, 256)
@@ -568,10 +593,21 @@
         for n, m in enumerate(places):
             proj_out[:, m, :] = total[:, n * 128:(n + 1) * 128] * rssq[m:m + 1, low_half]
 
-    inputs_arrived(1)
-    turn(t, 1)
-    other_arrived(1)
-    turn(1 - t, 1)
+    def piece(k):
+        return (1 - xl) * NY + lax.rem(y + k, NY)
+
+    def piece_copy(k):
+        ref = xr.at[t, piece(k)]
+        return remote(ref, ref, piece_send.at[k], piece_recv.at[k], sibling)
+
+    order = (0, 1, 3, 2)
+    for k in order:
+        arrived(xr.at[t, piece(k)], a_recv.at[piece(k)])
+        piece_copy(k).start()
+        turn_piece(t, piece(k))
+    for k in order:
+        arrived(xr.at[1 - t, piece(k)], piece_recv.at[k])
+        turn_piece(1 - t, piece(k))
     m_arrived(0)
     outer(0)
     m_arrived(1)
@@ -629,17 +665,19 @@
             left(bas.at[0, 0, LOW], yf_send.at[n, p])
     def dp_left(k):
         left(xr.at[0, 0], a_send.at[k])
-        for part in range(2):
-            m_copy(part, k).wait_send()
 
     loop(1, NX * NY, dp_left)
     for part in range(2):
         x_copy(part).wait_send()
+        for copy in m_copies(part):
+            copy.wait_send()
     for k in range(1, NY):
         relay_copy(k).wait_send()
     for part in range(2):
         loop(1, NZ, lambda k: z_copy(part, k).wait_send())
-    for copy in (*hand_overs, give_a, give_b, give_s):
+    for k in range(NY):
+        piece_copy(k).wait_send()
+    for copy in (hand_overs[0], give_a, give_b, give_s):
         copy.wait_send()
 
 
@@ -669,8 +707,8 @@
         dma((10, 2)), dma((4, 2)), dma((5, 2)), dma((2,)),
         dma((5,)), dma((5,)), dma((5, 2)), dma((4, 2)), dma((1,)), dma((1,)),
         dma((2, 2)), dma((2, 2)), dma((4,)), dma((4,)), dma((2, 4)), dma((2, 4)), dma((2, NZ)), dma((2, NZ)),
-        dma((NX * NY,)), dma((NX * NY,)), dma((NY,)), dma((NY,)), dma((5,)), dma((5,)),
-        dma((2, NX * NY)), dma((2, NX * NY)), dma((2,)), dma((2,)), dma((2, NZ)), dma((2, NZ)),
+        dma((NX * NY,)), dma((NX * NY,)), dma((NY,)), dma((NY,)), dma((NY,)), dma((NY,)), dma((5,)), dma((5,)),
+        dma((2, NX * NY, 2)), dma((2, NX * NY, 2)), dma((2,)), dma((2,)), dma((2, NZ)), dma((2, NZ)),
     ]
     hbm = pl.BlockSpec(memory_space=pl.ANY)
     smem = pl.BlockSpec(memory_space=pltpu.SMEM)

time: 107 us -> 103 us (0.963); the launches traced: 107 us -> 101 us
  Pallas kernels: 103 us -> 97.6 us
    pallas_call x1, Pallas kernels: 103 us -> 97.6 us  [on_device(): pl.pallas_call(kernel, out_shape=(pltpu.VMEM((1, 128, 2048), BF16), pltpu...]
where the time goes in v4:
time: 103 us; the launch traced here: 101 us
  Pallas kernels  97.6 us (95%)
  local copies, waits for them, and re-layouts  2.9 us (3%)
    pallas_call x1, Pallas kernels, on_device(): pl.pallas_call(kernel, out_shape=(pltpu.VMEM((1, 128, 2048), BF16), pltpu...  97.6 us
    unnamed x4, local copies, waits for them, and re-layouts  2.9 us

profile of v4, /device:TPU:6, one launch (start us, length us, event | category | flops | bytes accessed | tf_op | source)
XLA Modules:
  0.0 101.1 jit_solution(12809929462871682136)
XLA Ops:
  0.6 97.6 %shard_map.120 = (bf16[1,128,2048]{2,1,0:T(8,128)(2,1)S(1)}, bf16[1,128,2048]{2,1,0:T(8,128)(2,1)S(1)}, bf16[2,1,128,256]{3,2,1,0:T(8,128)(2,1)S(1)}, f32[64,4,128]{2,1,0:T(4,128)S(1)}) custom-call(bf16[1,128,8192]{2,1,0:T(8,128)(2,1)} %x_ref.1, bf16[1,128,2048]{2,1,0:T(8,128)(2,1)} %q_ref.1, bf16[2,1,128,256]{3,2,1,0:T(8,128)(2,1)} %kv_ref.1, ...), custom_call_target="tpu_custom_call" | custom-call | flops 7000000000 | bytes 12000000 | tf_op jit(solution)/shard_map/pallas_call | solution.py:715
  98.2 0.8 copy.17
  99.0 0.7 copy.19
  99.7 0.7 copy.20
  100.3 0.8 copy.18

commit v5 on v4

--- a/solution.py
+++ b/solution.py
@@ -216,7 +216,7 @@
     def side(dx):
         return xl if dx == 0 else 1 - xl
 
-    send_inputs(((1, 0), (3, 0), (0, 0), (1, 1), (3, 1)))
+    send_inputs(((1, 0), (3, 0), (0, 0)))
 
     def split_heads(h):
         g, i = lax.div(h, 8), lax.rem(h, 8)
@@ -319,6 +319,7 @@
         @pl.when(s == 2)
         def _():
             pick_x()
+            send_inputs(((1, 1), (3, 1)))
 
     loop(1, 5, forward_step)
     pick_y()

time: 103 us -> 102 us (level)
  no operation moved by 1% of the time
where the time goes in v5:
time: 102 us; the launch traced here: 100 us
  Pallas kernels  96.9 us (95%)
  local copies, waits for them, and re-layouts  2.9 us (3%)
    pallas_call x1, Pallas kernels, on_device(): pl.pallas_call(kernel, out_shape=(pltpu.VMEM((1, 128, 2048), BF16), pltpu...  96.9 us
    unnamed x4, local copies, waits for them, and re-layouts  2.9 us

profile of v5, /device:TPU:6, one launch (start us, length us, event | category | flops | bytes accessed | tf_op | source)
XLA Modules:
  0.0 100.4 jit_solution(3979383574900774141)
XLA Ops:
  0.6 96.9 %shard_map.120 = (bf16[1,128,2048]{2,1,0:T(8,128)(2,1)S(1)}, bf16[1,128,2048]{2,1,0:T(8,128)(2,1)S(1)}, bf16[2,1,128,256]{3,2,1,0:T(8,128)(2,1)S(1)}, f32[64,4,128]{2,1,0:T(4,128)S(1)}) custom-call(bf16[1,128,8192]{2,1,0:T(8,128)(2,1)} %x_ref.1, bf16[1,128,2048]{2,1,0:T(8,128)(2,1)} %q_ref.1, bf16[2,1,128,256]{3,2,1,0:T(8,128)(2,1)} %kv_ref.1, ...), custom_call_target="tpu_custom_call" | custom-call | flops 7000000000 | bytes 12000000 | tf_op jit(solution)/shard_map/pallas_call | solution.py:716
  97.5 0.8 copy.17
  98.3 0.7 copy.19
  99.0 0.7 copy.20
  99.6 0.8 copy.18
